TPU v7x, 256 devices: a whole 4x4x8 slice. The times are simulated.
256 devices in a mesh: stream: 8 (over x_lo, y), wall: 32 (over x_hi, z, core).
Axes of the slice: x: 4 (x_hi: 2, x_lo: 2; x = x_hi * 2 + x_lo), y: 4, z: 8, core: 2. Of those that a mesh axis runs over, the one named last changes fastest.
Arguments:
- right_side: float32 [2048, 24576], P('stream', 'wall'), may hold values from -6 to 6
- diagonal: float32 [2048, 24576], P('stream', 'wall'), may hold values from 0.05 to 1
- coarse_inverse: float32 [4096, 4096], P('wall', 'stream'), may hold values from -1 to 2
- owner_slot: int32 [256], replicated, may hold values from 0 to 255, each once
Outputs:
- pressure_update: float32 [2048, 24576], P('stream', 'wall')
- residual_field: float32 [2048, 24576], P('stream', 'wall')
All inputs are finite; a program needn't handle non-finite values.
Results may differ from a plain program's by a relative error of at most 0.0003.
Values sent between devices are 32-bit elements; how exact they have to be, the bound alone decides.
A program may use at most 64 MiB of HBM per device.

v0:
```python
import math

import jax
import jax.numpy as jnp
from jax import lax
from jax.sharding import PartitionSpec as P

MARGIN = 4
DEG = 4
MODES_X = 4
MODES_Y = 4


lower_end = 0.05
upper_end = 5.0
centre_weight = 8.0 / 3.0
side_weight = 1.0 / 3.0
precise = lax.Precision.HIGHEST


def padded_2(cells, sides, width):
    for axis, dim in sides:
        count = lax.axis_size(axis)
        head = lax.slice_in_dim(cells, 0, width, axis=dim)
        tail = lax.slice_in_dim(cells, cells.shape[dim] - width, cells.shape[dim], axis=dim)
        cells = jnp.concatenate(
            [
                lax.ppermute(tail, axis, [(i, (i + 1) % count) for i in range(count)]),
                cells,
                lax.ppermute(head, axis, [((i + 1) % count, i) for i in range(count)]),
            ],
            axis=dim,
        )
    return cells


def stencil(padded, shift):
    centre = padded[1:-1, 1:-1]
    beside_all = padded[:-2, :-2] + padded[:-2, 1:-1] + padded[:-2, 2:] + padded[1:-1, :-2]
    beside_all = beside_all + padded[1:-1, 2:] + padded[2:, :-2] + padded[2:, 1:-1] + padded[2:, 2:]
    return (centre_weight + shift) * centre - side_weight * beside_all


def chebyshev(source, shift, inside):
    middle = (upper_end + lower_end) / 2.0
    spread = (upper_end - lower_end) / 2.0
    quotient = middle / spread
    factor = 1.0 / quotient
    update = inside * source / middle
    estimate = update
    for sweep in range(DEG):
        defect = source - stencil(jnp.pad(estimate, 1), shift)
        factor_next = 1.0 / (2.0 * quotient - factor)
        update = inside * (factor_next * factor * update + 2.0 * factor_next / spread * defect)
        estimate = estimate + update
        factor = factor_next
    return estimate


def cosine_table(length, modes):
    position = jnp.arange(length, dtype=jnp.float32) + 0.5
    frequency = jnp.arange(modes, dtype=jnp.float32)
    return jnp.cos(jnp.pi * position[:, None] * frequency[None, :] / length)


def restrict(region, stream_table, wall_table):
    partial_product = jnp.dot(region, wall_table, precision=precise)
    scale = 1.0 / math.sqrt(stream_table.shape[0] * wall_table.shape[0])
    return jnp.dot(stream_table.T, partial_product, precision=precise) * scale


def prolong(coefficients, stream_table, wall_table):
    return jnp.dot(
        jnp.dot(stream_table, coefficients, precision=precise), wall_table.T, precision=precise
    )


def local(right_side, diagonal, coarse_inverse, owner_slot):
    rows_here = right_side.shape[0]
    cols_here = right_side.shape[1]
    stream_count = lax.axis_size("stream")
    wall_count = lax.axis_size("wall")
    stream_at = lax.axis_index("stream")
    wall_at = lax.axis_index("wall")
    subdomains = stream_count * wall_count
    mode_count = MODES_X * MODES_Y
    stream_table = cosine_table(rows_here, MODES_X)
    wall_table = cosine_table(cols_here, MODES_Y)
    my_slot = lax.dynamic_index_in_dim(
        owner_slot, stream_at * wall_count + wall_at, 0, keepdims=False
    )

    def rim_mask(depth):
        columns = wall_at * cols_here - depth + jnp.arange(cols_here + 2 * depth, dtype=jnp.int32)
        return ((columns >= 0) & (columns < cols_here * wall_count)).astype(jnp.float32)[None, :]

    mask_wide = rim_mask(MARGIN)
    stacked = jnp.stack([right_side, diagonal])
    extended = padded_2(stacked, (("stream", 1), ("wall", 2)), MARGIN)
    extended = extended * mask_wide[None]
    source_wide = extended[0]
    shift_wide = extended[1]
    full_rows = lax.all_gather(coarse_inverse, "stream", axis=1, tiled=True)

    def solve_coarse(coefficients):
        gathered = lax.all_gather(coefficients[None, :], ("stream", "wall"), axis=0, tiled=True)
        ordered = jnp.zeros((subdomains, mode_count), jnp.float32).at[owner_slot].set(gathered)
        ordered = ordered.reshape(subdomains * mode_count)
        partial_value = jnp.dot(full_rows, ordered, precision=precise)
        values = lax.all_gather(partial_value, "wall", axis=0, tiled=True)
        mine = lax.dynamic_slice_in_dim(values, my_slot * mode_count, mode_count)
        return mine.reshape(MODES_X, MODES_Y)

    def precondition(source_ext, shift_ext):
        solved = chebyshev(source_ext, shift_ext, mask_wide)
        owned = solved[MARGIN : MARGIN + rows_here, MARGIN : MARGIN + cols_here]
        owned_source = source_ext[MARGIN : MARGIN + rows_here, MARGIN : MARGIN + cols_here]
        coefficients = restrict(owned_source, stream_table, wall_table).reshape(mode_count)
        return owned + prolong(solve_coarse(coefficients), stream_table, wall_table)

    initial = precondition(source_wide, shift_wide)
    bordered = padded_2(initial, (("stream", 0), ("wall", 1)), 1) * rim_mask(1)
    residual_field = right_side - stencil(bordered, diagonal)
    next_wide = padded_2(residual_field, (("stream", 0), ("wall", 1)), MARGIN) * mask_wide
    second = precondition(next_wide, shift_wide)
    return (initial + second, residual_field)


def solution(mesh):
    placed = (P("stream", "wall"), P("stream", "wall"), P("wall", "stream"), P())
    return jax.shard_map(
        local,
        mesh=mesh,
        in_specs=placed,
        out_specs=(P("stream", "wall"), P("stream", "wall")),
        check_vma=False,
    )
```

profile of v0, /device:TPU:1, one launch (start us, length us, event | category | flops | bytes accessed | tf_op | source)
XLA Modules:
  0.0 893.2 jit_solution(18121609839339872806)
XLA Ops:
  8.7 4.6 collective-permute-start.1
  14.2 3.8 collective-permute-done
  18.2 2.2 collective-permute-start.3
  20.4 1.6 collective-permute-start.2
  23.4 2.7 collective-permute-done.3
  27.6 1.7 maximum_multiply_fusion
  30.4 2.3 fusion.15
  33.7 355.9 %all-gather = f32[256,1,16]{2,1,0:T(1,128)} all-gather(f32[1,1,16]{2,1,0:T(1,128)S(1)} %reshape.78), channel_id=1, replica_groups=mesh['stream'=8,'wall'=32] {'stream','wall'}, dimensions={0}, use_global_device_ids=true | all-gather | bytes 16448 | tf_op jit(solution)/shard_map/all_gather | solution.py:106
  389.6 2.6 scatter_custom_fusion
  393.3 1.7 fusion.60
  395.0 1.6 fusion.59
  396.6 3.0 fusion.26
  400.5 2.6 add_multiply_fusion.4
  403.1 3.3 convolution_bitcast_fusion.1
  406.4 38.8 %all-gather.1 = f32[32,1,128]{2,1,0:T(1,128)S(1)} all-gather(f32[1,1,128]{2,1,0:T(1,128)S(1)} %convolution_bitcast_fusion.1), channel_id=1, replica_groups=mesh['stream'=8,'wall'=32] {'wall'}, dimensions={0}, use_global_device_ids=true | all-gather | bytes 16896 | tf_op jit(solution)/shard_map/all_gather | solution.py:110
  446.0 5.3 convolution_add_fusion.1
  452.2 1.6 collective-permute-start.4
  454.6 2.4 collective-permute-done.4
  459.9 2.7 collective-permute-done.7
  462.6 1.5 maximum_multiply_fusion.1
  465.5 1.5 collective-permute-start.8
  468.0 2.2 collective-permute-done.8
  470.4 6.3 collective-permute-start.11
  480.0 2.3 fusion.13
  483.2 343.5 %all-gather.2 = f32[256,1,16]{2,1,0:T(1,128)S(1)} all-gather(f32[1,1,16]{2,1,0:T(1,128)S(1)} %reshape.82), channel_id=1, replica_groups=mesh['stream'=8,'wall'=32] {'stream','wall'}, dimensions={0}, use_global_device_ids=true | all-gather | bytes 16448 | tf_op jit(solution)/shard_map/all_gather | solution.py:106
  828.0 3.3 convolution_bitcast_fusion
  831.3 38.2 %all-gather.3 = f32[32,1,128]{2,1,0:T(1,128)S(1)} all-gather(f32[1,1,128]{2,1,0:T(1,128)S(1)} %convolution_bitcast_fusion), channel_id=1, replica_groups=mesh['stream'=8,'wall'=32] {'wall'}, dimensions={0}, use_global_device_ids=true | all-gather | bytes 16896 | tf_op jit(solution)/shard_map/all_gather | solution.py:110
  870.3 6.2 fusion.58
  876.5 1.6 fusion.57
  878.1 1.8 fusion.25
  879.9 1.6 add_multiply_fusion
  881.5 4.6 fusion
  (64 shorter events, 23.2 us)
Async XLA Ops:
  7.2 10.9 %copy-start = (f32[256,768]{1,0:T(8,128)S(1)}, f32[256,768]{1,0:T(8,128)}, u32[]{:S(2)}) copy-start(f32[256,768]{1,0:T(8,128)} %param.5) | copy-start | bytes 2359300
  7.2 10.9 %copy-start.1 = (f32[256,768]{1,0:T(8,128)S(1)}, f32[256,768]{1,0:T(8,128)}, u32[]{:S(2)}) copy-start(f32[256,768]{1,0:T(8,128)} %param.4) | copy-start | bytes 2359300
  7.2 6.1 copy-start.8
  7.2 395.9 %all-gather.6.cloned.1.call-start = ((), (), s32[]{:S(2)}) async-start(), calls=%async_computation | async-start | bytes 2359296 | tf_op jit(solution)/shard_map/all_gather | solution.py:103
  8.7 5.5 collective-permute-start.1
  13.3 4.8 collective-permute-start
  18.2 7.8 collective-permute-start.3
  20.4 7.2 collective-permute-start.2
  26.1 0.7 copy-start.7
  29.5 1.0 copy-start.6
  399.6 1.0 copy-start.3
  451.3 0.9 copy-start.4
  452.2 2.4 collective-permute-start.5
  452.2 4.8 collective-permute-start.4
  458.1 4.5 collective-permute-start.7
  459.5 3.1 collective-permute-start.6
  465.4 14.6 %copy-start.2 = (f32[256,768]{1,0:T(8,128)}, f32[256,768]{1,0:T(8,128)S(1)}, u32[]{:S(2)}) copy-start(f32[256,768]{1,0:T(8,128)S(1)} %fusion.8) | copy-start | bytes 2359300
  465.4 2.6 collective-permute-start.9
  465.5 4.7 collective-permute-start.8
  470.4 7.3 collective-permute-start.11
  476.6 2.0 collective-permute-start.10
  879.9 1.6 copy-start.5
Sparse Core Ops, SparseCore 0:
  9.8 46.1 all-gather.5
where the time goes:
time: 901 us; the launch traced here: 893 us
  blocking collectives  776 us (86%)
  other arithmetic  28.1 us (3%)
  matrix products  24.2 us (3%)
  waiting for transfers between devices  20.1 us (2%)
  starting transfers between devices  19.7 us (2%)
  between operations  15.2 us (2%)
  local copies, waits for them, and re-layouts  9.61 us (1%)
    all_gather x2, blocking collectives, solve_coarse(): lax.all_gather(coefficients[None, :], ('stream', 'wall'), axis=0, tiled=T...  699 us
    all_gather x2, blocking collectives, solve_coarse(): values = lax.all_gather(partial_value, 'wall', axis=0, tiled=True)  76.9 us
  transfers between devices with their start and end apart: 13, of which 11 were waited for; matrix products, arithmetic and copies ran while one was open for 2% of the time, Pallas kernels for 0%

commit v1 on v0

v1 whole, which is shorter than its diff:
```python
import math

import jax
import jax.numpy as jnp
import numpy as np
from jax import lax
from jax.experimental import pallas as pl
from jax.experimental.pallas import tpu as pltpu
from jax.sharding import PartitionSpec as P

MESH = pl.DeviceIdType.MESH
NS, NW = 8, 32
DEVICES = NS * NW
CX, CY = 256, 768
DEG = 4
ROWS, COLS = CX + 16, CY + 128
STRIPS = ROWS // 8
MIDDLE = (5.0 + 0.05) / 2.0
SPREAD = (5.0 - 0.05) / 2.0
SCALE = 1.0 / math.sqrt(CX * CY)
F32, BF16 = jnp.float32, jnp.bfloat16


def sweep_factors():
    quotient = MIDDLE / SPREAD
    factor = 1.0 / quotient
    pairs = []
    for _ in range(DEG):
        following = 1.0 / (2.0 * quotient - factor)
        pairs.append((following * factor, 2.0 * following / SPREAD))
        factor = following
    return pairs


def halves(table):
    high = table.astype(BF16)
    return high, (table - high.astype(np.float32)).astype(BF16)


def tables():
    phi = np.cos(np.pi * (np.arange(CX) + 0.5)[None, :] * np.arange(4)[:, None] / CX)
    psi = np.cos(np.pi * (np.arange(CY) + 0.5)[None, :] * np.arange(4)[:, None] / CY)
    phi_lanes = np.repeat(phi[1:].reshape(3 * CX, 1), 128, axis=1).astype(np.float32)
    psi_rows = np.concatenate([psi, psi]).astype(np.float32)
    stream = np.zeros((ROWS, 32), np.float32)
    stream[0:8, 0:4] = phi[:, CX - 8 :].T
    stream[8 : 8 + CX, 8:12] = phi.T
    stream[8 + CX :, 16:20] = phi[:, :8].T
    high, low = halves(stream)
    stream_k = np.concatenate([high, high, low, np.zeros_like(high)], axis=1)
    own_k = stream_k[8 : 8 + CX]
    wall = np.zeros((64, COLS), np.float32)
    for m in range(4):
        wall[4 * m : 4 * m + 4, COLS - 64 :] = psi[:, CY - 64 :]
        wall[16 + 4 * m : 20 + 4 * m, :CY] = psi
        wall[32 + 4 * m : 36 + 4 * m, CY : CY + 64] = psi[:, :64]
    high, low = halves(wall)
    wall_k = np.concatenate([high, high, low, np.zeros_like(high)], axis=0)
    return phi_lanes, psi_rows, stream_k, own_k, wall_k


def iota(shape, dim):
    return lax.broadcasted_iota(jnp.int32, shape, dim)


def split(value):
    high = value.astype(BF16).astype(F32)
    return high, value - high


def lane_totals(value):
    high, low = split(value)
    both = jnp.concatenate([high, low], axis=1).astype(BF16)
    return jnp.dot(both, jnp.ones((256, 128), BF16), preferred_element_type=F32)


def strip(i):
    return pl.ds(pl.multiple_of(i * 8, 8), 8)


def kernel(
    rhs_hbm, diag_hbm, inv_hbm, slot_hbm, slots_hbm, phi_hbm, psi_hbm, sk_hbm, so_hbm, wk_hbm,
    out_hbm, resid_hbm,
    ext, gm, d3, x, u, first, res, py, inv, phi, psi, sk, so, wk, slots,
    colsend, colrecv, corners, hcolsend, hcolrecv, hcorners, hrows,
    rows, bufs, ypk, slot,
    load_sem, msend, mrecv, asend, arecv, store_sem,
):
    s = lax.axis_index("stream")
    w = lax.axis_index("wall")
    me = s * NW + w
    ya, xl = s % 4, s // 4
    xh, za, core = w // 16, (w // 2) % 8, w % 2
    xa = xh * 2 + xl
    up, down = (s + NS - 1) % NS, (s + 1) % NS
    left, right = (w + NW - 1) % NW, (w + 1) % NW

    def around(k, n):
        return n // 2 + (k % 2) * ((k + 1) // 2) - (1 - k % 2) * (k // 2)

    def everyone(act):
        ys = [(ya + d) % 4 for d in (2, 3, 1, 0)]

        def some(k, count):
            z = (za + around(k // 4, 8)) % 8
            xx = (xa + around(k % 4, 4)) % 4
            base_s = (xx % 2) * 4
            base_w = (xx // 2) * 16 + z * 2
            for j in range(count):
                act((base_s + ys[j // 2], base_w + ((1 - core) if j % 2 == 0 else core)))

        def body(k, carry):
            some(k, 8)
            return carry

        lax.fori_loop(0, 31, body, 0)
        some(jnp.int32(31), 7)

    barrier = pltpu.get_barrier_semaphore()
    everyone(lambda to: pl.semaphore_signal(barrier, inc=1, device_id=to, device_id_type=MESH))

    own = ext.at[:, pl.ds(8, CX), pl.ds(0, CY)]
    loads = [
        pltpu.make_async_copy(src, dst, load_sem.at[i])
        for i, (src, dst) in enumerate(
            [
                (rhs_hbm, own.at[0]),
                (phi_hbm, phi),
                (psi_hbm, psi),
                (diag_hbm, own.at[1]),
                (slot_hbm, slot),
                (slots_hbm, slots),
                (inv_hbm, inv),
                (sk_hbm, sk),
                (so_hbm, so),
                (wk_hbm, wk),
            ]
        )
    ]
    for load in loads:
        load.start()

    lane = iota((8, 128), 1)
    sub = iota((8, 128), 0)
    lane16 = iota((16, 128), 1)

    def restrict(ref):
        def body(i, sums):
            f = ref[strip(i + 1), 0:CY]
            new = [sums[0] + f]
            for m in range(3):
                t = phi[pl.ds(pl.multiple_of(m * CX + i * 8, 8), 8), :]
                new.append(sums[m + 1] + f * jnp.concatenate([t] * 6, axis=1))
            return tuple(new)

        zero = jnp.zeros((8, CY), F32)
        sums = lax.fori_loop(0, CX // 8, body, (zero,) * 4)
        parts = []
        for m in range(4):
            for n in range(4):
                value = sums[m] if n == 0 else sums[m] * psi[n : n + 1, :]
                total = value[:, 0:128]
                for t in range(1, 6):
                    total = total + value[:, 128 * t : 128 * t + 128]
                parts.append(total)
        totals = lane_totals(jnp.concatenate(parts, axis=0))
        keep = iota((128, 128), 0) // 8 == iota((128, 128), 1) % 16
        return jnp.sum(jnp.where(keep, totals, 0.0), axis=0, keepdims=True) * SCALE

    def pack(ref):
        to_left = jnp.zeros((16, 128), F32)
        to_right = jnp.zeros((16, 128), F32)
        for k in range(16):
            a = jnp.where(lane16 < 8, ref[8 + 16 * k : 24 + 16 * k, 0:128], 0.0)
            b = jnp.where(lane16 >= 120, ref[8 + 16 * k : 24 + 16 * k, CY - 128 : CY], 0.0)
            to_left = to_left + (pltpu.roll(a, 8 * k, 1) if k else a)
            shift = (8 * k + 8) % 128
            to_right = to_right + (pltpu.roll(b, shift, 1) if shift else b)
        return to_left, to_right

    def unpack(from_right, from_left, k):
        a = pltpu.roll(from_right, 128 - 8 * k, 1) if k else from_right
        shift = (120 - 8 * k) % 128
        b = pltpu.roll(from_left, shift, 1) if shift else from_left
        return jnp.where(lane16 < 8, a, jnp.where(lane16 >= 120, b, 0.0))

    def corner(from_right, from_left):
        return jnp.where(lane < 8, from_right, jnp.where(lane >= 120, from_left, 0.0))

    def to_neighbours(which, pairs):
        targets = [(up, w), (down, w), (s, left), (s, right), (up, left), (up, right), (down, left), (down, right)]
        return [
            pltpu.make_async_remote_copy(
                src_ref=src, dst_ref=dst, send_sem=msend.at[which, i], recv_sem=mrecv.at[which, i],
                device_id=to, device_id_type=MESH,
            )
            for i, ((src, dst), to) in enumerate(zip(pairs, targets, strict=True))
        ]

    def send_row(which):
        def act(to):
            pltpu.make_async_remote_copy(
                src_ref=rows.at[which, pl.ds(0, 1)], dst_ref=bufs.at[which, pl.ds(me, 1)],
                send_sem=asend.at[which], recv_sem=arecv.at[which], device_id=to, device_id_type=MESH,
            ).start()

        everyone(act)
        pltpu.make_async_copy(
            rows.at[which, pl.ds(0, 1)], bufs.at[which, pl.ds(me, 1)], arecv.at[which]
        ).start()

    def wait_rows(which):
        pltpu.make_async_copy(bufs.at[which], bufs.at[which], arecv.at[which]).wait()

    def wait_sent(which):
        part = bufs.at[which, pl.ds(0, DEVICES - 1)]
        pltpu.make_async_copy(part, part, asend.at[which]).wait()

    def partial_values(c):
        at = iota((32, DEVICES), 0) + 32 * s
        pick = jnp.where(slots[...] == at, 1.0, 0.0)
        high, low = split(c)
        pick2 = jnp.concatenate([pick, pick], axis=1).astype(BF16)
        both = jnp.concatenate([high, low], axis=0).astype(BF16)
        ordered = jnp.dot(pick2, both, preferred_element_type=F32)
        keep = iota((32, 128), 1) // 16 == iota((32, 128), 0) % 8
        ordered = jnp.where(keep, ordered, 0.0)
        total = jnp.zeros((128, 128), F32)
        for q in range(4):
            row = jnp.sum(ordered[8 * q : 8 * q + 8], axis=0, keepdims=True)
            total = total + inv[:, 128 * q : 128 * q + 128] * row
        sums = lane_totals(total)
        return jnp.sum(jnp.where(iota((128, 128), 0) == iota((128, 128), 1), sums, 0.0), axis=0, keepdims=True)

    def add_partials(which):
        total = bufs[2 * which + 1, 0:32]
        for a in range(1, NS):
            total = total + bufs[2 * which + 1, 32 * a : 32 * a + 32]
        ypk[which] = total

    def coefficients(which, a, b, place):
        mine = slot[a * NW + b]
        row = ypk[which, pl.ds(lax.shift_right_logical(mine, 3), 1), :]
        shift = lax.bitwise_and(16 * place + 128 - 16 * lax.bitwise_and(mine, 7), 127)
        rolled = pltpu.roll(jnp.broadcast_to(row, (8, 128)), shift, 1)
        return jnp.where(lane // 16 == place, rolled, 0.0)

    def prolonged(groups, stream_table, wall_table):
        own_row = (lane % 16) // 4 == sub
        stacked = jnp.concatenate(
            [jnp.where(own_row, g, 0.0) for g in groups] + [jnp.zeros((8, 128), F32)], axis=0
        )
        high, low = split(stacked)
        operand = jnp.concatenate([high + pltpu.roll(low, 64, 1), high], axis=1).astype(BF16)
        mixed = jnp.dot(operand, wall_table, preferred_element_type=F32)
        high, low = split(mixed)
        operand = jnp.concatenate([high, low, high, jnp.zeros_like(high)], axis=0).astype(BF16)
        return jnp.dot(stream_table[...], operand, preferred_element_type=F32)

    tail_lane = iota((8, 128), 1)

    def tail_valid(depth):
        inner = jnp.logical_and(tail_lane < depth, w < NW - 1)
        outer = jnp.logical_and(tail_lane >= 128 - depth, w > 0)
        return jnp.logical_or(inner, outer)

    def masked(value, valid):
        return jnp.concatenate([value[:, 0:CY], jnp.where(valid, value[:, CY:], 0.0)], axis=1)

    wide_sub = iota((8, COLS), 0)

    def hsum(v):
        return v + pltpu.roll(v, 1, 1) + pltpu.roll(v, COLS - 1, 1)

    def vsum(before, here, after):
        above = pltpu.roll(jnp.where(wide_sub == 7, before, here), 1, 0)
        below = pltpu.roll(jnp.where(wide_sub == 0, after, here), 7, 0)
        return here + above + below

    def chebyshev(g):
        valid = tail_valid(4)

        def begin(i, carry):
            value = g[strip(i), :] * (1.0 / MIDDLE)
            x[strip(i), :] = value
            u[strip(i), :] = value
            return carry

        lax.fori_loop(0, STRIPS, begin, 0)
        for a, b in sweep_factors():

            def update(i, total):
                here = x[strip(i), :]
                e = g[strip(i), :] - d3[strip(i), :] * here + total * (1.0 / 3.0)
                return here, masked(a * u[strip(i), :] + b * e, valid)

            h0 = hsum(x[0:8, :])
            h1 = hsum(x[8:16, :])
            here, step = update(0, vsum(jnp.zeros_like(h0), h0, h1))
            step = jnp.where(wide_sub >= 4, step, 0.0)
            u[0:8, :] = step
            x[0:8, :] = here + step

            def body(i, carry):
                before, now = carry
                after = hsum(x[strip(i + 1), :])
                here, step = update(i, vsum(before, now, after))
                u[strip(i), :] = step
                x[strip(i), :] = here + step
                return now, after

            before, now = lax.fori_loop(1, STRIPS - 1, body, (h0, h1))
            here, step = update(STRIPS - 1, vsum(before, now, jnp.zeros_like(now)))
            step = jnp.where(wide_sub < 4, step, 0.0)
            u[ROWS - 8 : ROWS, :] = step
            x[ROWS - 8 : ROWS, :] = here + step

    loads[0].wait()
    loads[1].wait()
    loads[2].wait()
    rows[0] = jnp.broadcast_to(restrict(ext.at[0]), (8, 128))
    loads[3].wait()
    for f in range(2):
        a, b = pack(ext.at[f])
        colsend[0, 16 * f : 16 * f + 16] = a
        colsend[1, 16 * f : 16 * f + 16] = b

    pl.semaphore_wait(barrier, DEVICES - 1)
    top, bottom = pl.ds(8, 8), pl.ds(CX, 8)
    west, east, body_lanes = pl.ds(0, 128), pl.ds(CY - 128, 128), pl.ds(0, CY)
    margins = to_neighbours(
        0,
        [
            (ext.at[:, top, body_lanes], ext.at[:, pl.ds(ROWS - 8, 8), body_lanes]),
            (ext.at[:, bottom, body_lanes], ext.at[:, pl.ds(0, 8), body_lanes]),
            (colsend.at[0], colrecv.at[0]),
            (colsend.at[1], colrecv.at[1]),
            (ext.at[:, top, west], corners.at[3]),
            (ext.at[:, top, east], corners.at[2]),
            (ext.at[:, bottom, west], corners.at[1]),
            (ext.at[:, bottom, east], corners.at[0]),
        ],
    )
    for copy in margins:
        copy.start()
    send_row(0)
    for copy in margins:
        copy.wait_recv()

    valid4 = tail_valid(4)
    for f in range(2):
        from_right = colrecv[0, 16 * f : 16 * f + 16]
        from_left = colrecv[1, 16 * f : 16 * f + 16]
        for k in range(16):
            ext[f, 8 + 16 * k : 24 + 16 * k, CY:COLS] = unpack(from_right, from_left, k)
        ext[f, 0:8, CY:COLS] = corner(corners[1, f], corners[0, f])
        ext[f, ROWS - 8 : ROWS, CY:COLS] = corner(corners[3, f], corners[2, f])

    def prepare(i, carry):
        gm[strip(i), :] = masked(ext[0, strip(i), :], valid4)
        d3[strip(i), :] = ext[1, strip(i), :] + 3.0
        return carry

    lax.fori_loop(0, STRIPS, prepare, 0)
    gm[0:8, :] = jnp.where(wide_sub >= 4, gm[0:8, :], 0.0)
    gm[ROWS - 8 : ROWS, :] = jnp.where(wide_sub < 4, gm[ROWS - 8 : ROWS, :], 0.0)
    chebyshev(gm)

    a, b = pack(x)
    hcolsend[0] = a
    hcolsend[1] = b
    halos = to_neighbours(
        1,
        [
            (x.at[top, body_lanes], hrows.at[1]),
            (x.at[bottom, body_lanes], hrows.at[0]),
            (hcolsend.at[0], hcolrecv.at[0]),
            (hcolsend.at[1], hcolrecv.at[1]),
            (x.at[top, west], hcorners.at[3]),
            (x.at[top, east], hcorners.at[2]),
            (x.at[bottom, west], hcorners.at[1]),
            (x.at[bottom, east], hcorners.at[0]),
        ],
    )
    for copy in halos:
        copy.start()

    for load in loads[4:]:
        load.wait()
    wait_rows(0)
    rows[1] = jnp.broadcast_to(partial_values(bufs[0]), (8, 128))
    send_row(1)

    for copy in halos:
        copy.wait_recv()
    valid8 = tail_valid(8)

    def place(i, carry):
        first[strip(i), 0:CY] = x[strip(i), 0:CY]
        return carry

    lax.fori_loop(1, STRIPS - 1, place, 0)
    first[0:8, 0:CY] = hrows[0]
    first[ROWS - 8 : ROWS, 0:CY] = hrows[1]
    for k in range(16):
        edge = unpack(hcolrecv[0], hcolrecv[1], k)
        first[8 + 16 * k : 16 + 16 * k, CY:COLS] = jnp.where(valid8, edge[0:8], 0.0)
        first[16 + 16 * k : 24 + 16 * k, CY:COLS] = jnp.where(valid8, edge[8:16], 0.0)
    first[0:8, CY:COLS] = jnp.where(valid8, corner(hcorners[1], hcorners[0]), 0.0)
    first[ROWS - 8 : ROWS, CY:COLS] = jnp.where(valid8, corner(hcorners[3], hcorners[2]), 0.0)

    wait_rows(1)
    add_partials(0)
    groups = []
    for a in (up, s, down):
        group = coefficients(0, a, w, 1)
        group = group + jnp.where(w > 0, coefficients(0, a, left, 0), 0.0)
        group = group + jnp.where(w < NW - 1, coefficients(0, a, right, 2), 0.0)
        groups.append(group)
    py[...] = prolonged(groups, sk, wk[...])

    def total_at(i):
        value = first[strip(i), :] + py[strip(i), :]
        first[strip(i), :] = value
        return hsum(value)

    def residual(i, total):
        value = gm[strip(i), :] - d3[strip(i), :] * first[strip(i), :] + total * (1.0 / 3.0)
        return masked(value, valid4)

    h0 = total_at(0)
    h1 = total_at(1)
    res[0:8, :] = jnp.where(wide_sub >= 4, residual(0, vsum(jnp.zeros_like(h0), h0, h1)), 0.0)

    def residual_body(i, carry):
        before, now = carry
        after = total_at(i + 1)
        res[strip(i), :] = residual(i, vsum(before, now, after))
        return now, after

    before, now = lax.fori_loop(1, STRIPS - 1, residual_body, (h0, h1))
    res[ROWS - 8 : ROWS, :] = jnp.where(
        wide_sub < 4, residual(STRIPS - 1, vsum(before, now, jnp.zeros_like(now))), 0.0
    )

    rows[2] = jnp.broadcast_to(restrict(res), (8, 128))
    send_row(2)
    resid_copy = pltpu.make_async_copy(res.at[pl.ds(8, CX), pl.ds(0, CY)], resid_hbm, store_sem.at[0])
    resid_copy.start()
    for copy in halos:
        copy.wait_send()
    chebyshev(res)
    wait_rows(2)
    rows[3] = jnp.broadcast_to(partial_values(bufs[2]), (8, 128))
    send_row(3)

    def add_local(i, carry):
        first[strip(i), 0:CY] = first[strip(i), 0:CY] + x[strip(i), 0:CY]
        return carry

    lax.fori_loop(1, STRIPS - 1, add_local, 0)
    wait_rows(3)
    add_partials(1)
    none = jnp.zeros((8, 128), F32)
    py[0:CX, 0:CY] = prolonged([none, coefficients(1, s, w, 1), none], so, wk[:, 0:CY])

    def add_coarse(i, carry):
        first[strip(i + 1), 0:CY] = first[strip(i + 1), 0:CY] + py[strip(i), 0:CY]
        return carry

    lax.fori_loop(0, CX // 8, add_coarse, 0)
    out_copy = pltpu.make_async_copy(first.at[pl.ds(8, CX), pl.ds(0, CY)], out_hbm, store_sem.at[1])
    out_copy.start()
    for which in range(4):
        wait_sent(which)
    for copy in margins:
        copy.wait_send()
    resid_copy.wait()
    out_copy.wait()


def local(right_side, diagonal, coarse_inverse, owner_slot):
    phi_lanes, psi_rows, stream_k, own_k, wall_k = tables()
    field = jax.ShapeDtypeStruct((CX, CY), F32)
    anywhere = pl.BlockSpec(memory_space=pl.ANY)
    vmem = pltpu.VMEM
    dma = pltpu.SemaphoreType.DMA
    work = vmem((ROWS, COLS), F32)
    return pl.pallas_call(
        kernel,
        out_shape=(field, field),
        in_specs=[anywhere] * 10,
        out_specs=(anywhere, anywhere),
        scratch_shapes=[
            vmem((2, ROWS, COLS), F32), work, work, work, work, work, work, work,
            vmem((128, 512), F32), vmem((3 * CX, 128), F32), vmem((8, CY), F32),
            vmem((ROWS, 128), BF16), vmem((CX, 128), BF16), vmem((256, COLS), BF16), vmem((1, DEVICES), jnp.int32),
            vmem((2, 32, 128), F32), vmem((2, 32, 128), F32), vmem((4, 2, 8, 128), F32),
            vmem((2, 16, 128), F32), vmem((2, 16, 128), F32), vmem((4, 8, 128), F32), vmem((2, 8, CY), F32),
            vmem((4, 8, 128), F32), vmem((4, DEVICES, 128), F32), vmem((2, 32, 128), F32),
            pltpu.SMEM((DEVICES,), jnp.int32),
            dma((10,)), dma((2, 8)), dma((2, 8)), dma((4,)), dma((4,)), dma((2,)),
        ],
        compiler_params=pltpu.CompilerParams(
            collective_id=0, has_side_effects=True, vmem_limit_bytes=32 * 1024 * 1024
        ),
        cost_estimate=pl.CostEstimate(flops=100_000_000, bytes_accessed=4_000_000, transcendentals=0),
    )(
        right_side, diagonal, coarse_inverse, owner_slot, owner_slot.reshape(1, DEVICES),
        phi_lanes, psi_rows, stream_k, own_k, wall_k,
    )


def solution(mesh):
    placed = (P("stream", "wall"), P("stream", "wall"), P("wall", "stream"), P())
    return jax.shard_map(
        local,
        mesh=mesh,
        in_specs=placed,
        out_specs=(P("stream", "wall"), P("stream", "wall")),
        check_vma=False,
    )
```

time: 901 us -> 82.8 us (0.09)
  blocking collectives: 776 us -> 0 us
  Pallas kernels: 0 us -> 71.6 us
  other arithmetic: 28.1 us -> 0 us
  matrix products: 24.2 us -> 0 us
  waiting for transfers between devices: 20.1 us -> 0 us
  starting transfers between devices: 19.7 us -> 0 us
  between operations: 15.2 us -> 0.66 us
    all_gather x4 -> x0, blocking collectives: 776 us -> none  [the longest x2 699 us: solve_coarse(): lax.all_gather(coefficients[None, :], ('stream', 'wall'), axis=0, tiled=T...]
    pallas_call x0 -> x1, Pallas kernels: none -> 71.6 us  [local(): pl.pallas_call(kernel, out_shape=(field, field), in_specs=[anywhere] * 10...]
    dot_general x10 -> x0, matrix products: 24.2 us -> none  [the longest x2 9.9 us: prolong(): jnp.dot(jnp.dot(stream_table, coefficients, precision=precise), wall_tabl...]
    ppermute x12 -> x0, starting transfers between devices: 19.6 us -> none  [the longest x6 14.6 us: padded_2(): lax.ppermute(head, axis, [((i + 1) % count, i) for i in range(count)])]
    ppermute x12 -> x0, waiting for transfers between devices: 19.4 us -> none  [the longest x6 10.2 us: padded_2(): lax.ppermute(tail, axis, [(i, (i + 1) % count) for i in range(count)])]
    mul x8 -> x0, other arithmetic: 12.1 us -> none  [the longest x4 8.87 us: stencil(): return (centre_weight + shift) * centre - side_weight * beside_all]
    add x4 -> x0, other arithmetic: 11.1 us -> none  [chebyshev(): estimate = estimate + update]
  transfers between devices with their start and end apart: 13 -> 0, of which waited for: 11 -> 0; matrix products, arithmetic and copies ran while one was open for 2% -> 0% of each run, Pallas kernels for 0% -> 0%
where the time goes in v1:
time: 82.8 us; the launch traced here: 82.3 us
  Pallas kernels  71.6 us (86%)
  local copies, waits for them, and re-layouts  10.1 us (12%)
    pallas_call x1, Pallas kernels, local(): pl.pallas_call(kernel, out_shape=(field, field), in_specs=[anywhere] * 10...  71.6 us
    unnamed x20, local copies, waits for them, and re-layouts  10.1 us

profile of v1, /device:TPU:1, one launch (start us, length us, event | category | flops | bytes accessed | tf_op | source)
XLA Modules:
  0.0 82.3 jit_solution(9493942910884606038)
XLA Ops:
  0.6 0.0 copy-start.8
  0.6 0.7 copy-done.8
  1.3 0.0 copy-start
  1.3 1.1 %copy-done = f32[256,768]{1,0:T(8,128)S(1)} copy-done((f32[256,768]{1,0:T(8,128)S(1)}, f32[256,768]{1,0:T(8,128)}, u32[]{:S(2)}) %copy-start) | copy-done | bytes 786456
  2.4 0.0 copy-start.1
  2.4 1.1 %copy-done.1 = f32[256,768]{1,0:T(8,128)S(1)} copy-done((f32[256,768]{1,0:T(8,128)S(1)}, f32[256,768]{1,0:T(8,128)}, u32[]{:S(2)}) %copy-start.1) | copy-done | bytes 786456
  3.6 0.0 copy-start.2
  3.6 1.0 %copy-done.2 = bf16[256,896]{1,0:T(8,128)(2,1)S(1)} copy-done((bf16[256,896]{1,0:T(8,128)(2,1)S(1)}, bf16[256,896]{1,0:T(8,128)(2,1)}, u32[]{:S(2)}) %copy-start.2) | copy-done | bytes 458776
  4.6 0.0 copy-start.3
  4.6 1.0 %copy-done.3 = f32[768,128]{1,0:T(8,128)S(1)} copy-done((f32[768,128]{1,0:T(8,128)S(1)}, f32[768,128]{1,0:T(8,128)}, u32[]{:S(2)}) %copy-start.3) | copy-done | bytes 393240
  5.6 0.0 copy-start.4
  5.6 0.9 %copy-done.4 = f32[128,512]{1,0:T(8,128)S(1)} copy-done((f32[128,512]{1,0:T(8,128)S(1)}, f32[128,512]{1,0:T(8,128)}, u32[]{:S(2)}) %copy-start.4) | copy-done | bytes 262168
  6.5 0.0 copy-start.5
  6.5 0.9 %copy-done.5 = bf16[272,128]{1,0:T(8,128)(2,1)S(1)} copy-done((bf16[272,128]{1,0:T(8,128)(2,1)S(1)}, bf16[272,128]{1,0:T(8,128)(2,1)}, u32[]{:S(2)}) %copy-start.5) | copy-done | bytes 69656
  7.4 0.0 copy-start.6
  7.4 0.8 %copy-done.6 = bf16[256,128]{1,0:T(8,128)(2,1)S(1)} copy-done((bf16[256,128]{1,0:T(8,128)(2,1)S(1)}, bf16[256,128]{1,0:T(8,128)(2,1)}, u32[]{:S(2)}) %copy-start.6) | copy-done | bytes 65560
  8.3 0.0 copy-start.7
  8.3 0.7 copy-done.7
  9.0 71.6 %shard_map.104 = (f32[256,768]{1,0:T(8,128)S(1)}, f32[256,768]{1,0:T(8,128)S(1)}) custom-call(f32[256,768]{1,0:T(8,128)S(1)} %copy-done, f32[256,768]{1,0:T(8,128)S(1)} %copy-done.1, f32[128,512]{1,0:T(8,128)S(1)} %copy-done.4, s32[256]{0:T(256)S(1)} %copy-done.8, s32[1,256]{1,0:T(1,128)S(1)} %bitcast.1, f32[768,128]{1,0:T(8,128)S(1)} %copy-done.3, ...), custom_call_target="tpu_custom_call" | custom-call | flops 100000000 | bytes 4000000 | tf_op jit(solution)/shard_map/pallas_call | solution.py:489
  80.6 0.9 %copy.13 = f32[256,768]{1,0:T(8,128)} copy(f32[256,768]{1,0:T(8,128)S(1)} %get-tuple-element.4) | data formatting | bytes 1572864
  81.5 0.9 %copy.14 = f32[256,768]{1,0:T(8,128)} copy(f32[256,768]{1,0:T(8,128)S(1)} %get-tuple-element.5) | data formatting | bytes 1572864
Async XLA Ops:
  0.6 0.7 copy-start.8
  1.3 1.1 %copy-start = (f32[256,768]{1,0:T(8,128)S(1)}, f32[256,768]{1,0:T(8,128)}, u32[]{:S(2)}) copy-start(f32[256,768]{1,0:T(8,128)} %rhs_hbm.1) | copy-start | bytes 2359300
  2.4 1.1 %copy-start.1 = (f32[256,768]{1,0:T(8,128)S(1)}, f32[256,768]{1,0:T(8,128)}, u32[]{:S(2)}) copy-start(f32[256,768]{1,0:T(8,128)} %diag_hbm.1) | copy-start | bytes 2359300
  3.6 1.0 %copy-start.2 = (bf16[256,896]{1,0:T(8,128)(2,1)S(1)}, bf16[256,896]{1,0:T(8,128)(2,1)}, u32[]{:S(2)}) copy-start(bf16[256,896]{1,0:T(8,128)(2,1)} %constant.14.clone.wk_hbm) | copy-start | bytes 1376260
  4.6 1.0 %copy-start.3 = (f32[768,128]{1,0:T(8,128)S(1)}, f32[768,128]{1,0:T(8,128)}, u32[]{:S(2)}) copy-start(f32[768,128]{1,0:T(8,128)} %constant.10.clone.phi_hbm) | copy-start | bytes 1179652
  5.6 0.9 %copy-start.4 = (f32[128,512]{1,0:T(8,128)S(1)}, f32[128,512]{1,0:T(8,128)}, u32[]{:S(2)}) copy-start(f32[128,512]{1,0:T(8,128)} %inv_hbm.1) | copy-start | bytes 786436
  6.5 0.9 %copy-start.5 = (bf16[272,128]{1,0:T(8,128)(2,1)S(1)}, bf16[272,128]{1,0:T(8,128)(2,1)}, u32[]{:S(2)}) copy-start(bf16[272,128]{1,0:T(8,128)(2,1)} %constant.12.clone.sk_hbm) | copy-start | bytes 208900
  7.4 0.8 %copy-start.6 = (bf16[256,128]{1,0:T(8,128)(2,1)S(1)}, bf16[256,128]{1,0:T(8,128)(2,1)}, u32[]{:S(2)}) copy-start(bf16[256,128]{1,0:T(8,128)(2,1)} %constant.13.clone.so_hbm) | copy-start | bytes 196612
  8.3 0.7 copy-start.7

commit v2 on v1

--- a/solution.py
+++ b/solution.py
@@ -74,14 +74,24 @@
     return jnp.dot(both, jnp.ones((256, 128), BF16), preferred_element_type=F32)
 
 
+def prolonged(groups, stream_table, wall_table):
+    stacked = jnp.concatenate(groups + [jnp.zeros((8, 128), F32)], axis=0)
+    high, low = split(stacked)
+    operand = jnp.concatenate([high + pltpu.roll(low, 64, 1), high], axis=1).astype(BF16)
+    mixed = jnp.dot(operand, wall_table, preferred_element_type=F32)
+    high, low = split(mixed)
+    operand = jnp.concatenate([high, low, high, jnp.zeros_like(high)], axis=0).astype(BF16)
+    return jnp.dot(stream_table, operand, preferred_element_type=F32)
+
+
 def strip(i):
     return pl.ds(pl.multiple_of(i * 8, 8), 8)
 
 
 def kernel(
-    rhs_hbm, diag_hbm, inv_hbm, slot_hbm, slots_hbm, phi_hbm, psi_hbm, sk_hbm, so_hbm, wk_hbm,
-    out_hbm, resid_hbm,
-    ext, gm, d3, x, u, first, res, py, inv, phi, psi, sk, so, wk, slots,
+    rhs_hbm, diag_hbm, inv_hbm, slot_hbm, slots_hbm, phi_hbm, psi_hbm, sk_hbm, wk_hbm,
+    base_hbm, resid_hbm, mine_out,
+    ext, gm, d9, x, x2, u, first, res, py, inv, phi, psi, sk, wk, slots,
     colsend, colrecv, corners, hcolsend, hcolrecv, hcorners, hrows,
     rows, bufs, ypk, slot,
     load_sem, msend, mrecv, asend, arecv, store_sem,
@@ -132,7 +142,6 @@
                 (slots_hbm, slots),
                 (inv_hbm, inv),
                 (sk_hbm, sk),
-                (so_hbm, so),
                 (wk_hbm, wk),
             ]
         )
@@ -245,18 +254,6 @@
         rolled = pltpu.roll(jnp.broadcast_to(row, (8, 128)), shift, 1)
         return jnp.where(lane // 16 == place, rolled, 0.0)
 
-    def prolonged(groups, stream_table, wall_table):
-        own_row = (lane % 16) // 4 == sub
-        stacked = jnp.concatenate(
-            [jnp.where(own_row, g, 0.0) for g in groups] + [jnp.zeros((8, 128), F32)], axis=0
-        )
-        high, low = split(stacked)
-        operand = jnp.concatenate([high + pltpu.roll(low, 64, 1), high], axis=1).astype(BF16)
-        mixed = jnp.dot(operand, wall_table, preferred_element_type=F32)
-        high, low = split(mixed)
-        operand = jnp.concatenate([high, low, high, jnp.zeros_like(high)], axis=0).astype(BF16)
-        return jnp.dot(stream_table[...], operand, preferred_element_type=F32)
-
     tail_lane = iota((8, 128), 1)
 
     def tail_valid(depth):
@@ -277,43 +274,45 @@
         below = pltpu.roll(jnp.where(wide_sub == 0, after, here), 7, 0)
         return here + above + below
 
+    def rows_at(i):
+        return slice(8 * i, 8 * i + 8)
+
+    def stencil_strips(load, use):
+        zero = jnp.zeros((8, COLS), F32)
+        value = load(0)
+        before, now = zero, hsum(value)
+        for i in range(STRIPS):
+            following = load(i + 1) if i + 1 < STRIPS else None
+            after = zero if following is None else hsum(following)
+            use(i, value, vsum(before, now, after))
+            before, now, value = now, after, following
+
+    def inside(i, value, valid):
+        value = masked(value, valid)
+        if i == 0:
+            return jnp.where(wide_sub >= 4, value, 0.0)
+        if i == STRIPS - 1:
+            return jnp.where(wide_sub < 4, value, 0.0)
+        return value
+
     def chebyshev(g):
         valid = tail_valid(4)
-
-        def begin(i, carry):
-            value = g[strip(i), :] * (1.0 / MIDDLE)
-            x[strip(i), :] = value
-            u[strip(i), :] = value
-            return carry
-
-        lax.fori_loop(0, STRIPS, begin, 0)
-        for a, b in sweep_factors():
-
-            def update(i, total):
-                here = x[strip(i), :]
-                e = g[strip(i), :] - d3[strip(i), :] * here + total * (1.0 / 3.0)
-                return here, masked(a * u[strip(i), :] + b * e, valid)
-
-            h0 = hsum(x[0:8, :])
-            h1 = hsum(x[8:16, :])
-            here, step = update(0, vsum(jnp.zeros_like(h0), h0, h1))
-            step = jnp.where(wide_sub >= 4, step, 0.0)
-            u[0:8, :] = step
-            x[0:8, :] = here + step
-
-            def body(i, carry):
-                before, now = carry
-                after = hsum(x[strip(i + 1), :])
-                here, step = update(i, vsum(before, now, after))
-                u[strip(i), :] = step
-                x[strip(i), :] = here + step
-                return now, after
-
-            before, now = lax.fori_loop(1, STRIPS - 1, body, (h0, h1))
-            here, step = update(STRIPS - 1, vsum(before, now, jnp.zeros_like(now)))
-            step = jnp.where(wide_sub < 4, step, 0.0)
-            u[ROWS - 8 : ROWS, :] = step
-            x[ROWS - 8 : ROWS, :] = here + step
+        old, new = x, x2
+        for k, (a, b) in enumerate(sweep_factors()):
+
+            def load(i, k=k, old=old):
+                return g[rows_at(i), :] * (1.0 / (3.0 * MIDDLE)) if k == 0 else old[rows_at(i), :]
+
+            def use(i, value, total, k=k, a=a, b=b, new=new):
+                e = g[rows_at(i), :] - d9[rows_at(i), :] * value + total
+                step = a * (value if k == 0 else u[rows_at(i), :]) + (b / 3.0) * e
+                step = inside(i, step, valid)
+                if k < DEG - 1:
+                    u[rows_at(i), :] = step
+                new[rows_at(i), :] = value + step
+
+            stencil_strips(load, use)
+            old, new = new, old
 
     loads[0].wait()
     loads[1].wait()
@@ -358,10 +357,10 @@
 
     def prepare(i, carry):
         gm[strip(i), :] = masked(ext[0, strip(i), :], valid4)
-        d3[strip(i), :] = ext[1, strip(i), :] + 3.0
+        d9[strip(i), :] = ext[1, strip(i), :] * 3.0 + 9.0
         return carry
 
-    lax.fori_loop(0, STRIPS, prepare, 0)
+    lax.fori_loop(0, STRIPS, prepare, 0, unroll=True)
     gm[0:8, :] = jnp.where(wide_sub >= 4, gm[0:8, :], 0.0)
     gm[ROWS - 8 : ROWS, :] = jnp.where(wide_sub < 4, gm[ROWS - 8 : ROWS, :], 0.0)
     chebyshev(gm)
@@ -399,7 +398,7 @@
         first[strip(i), 0:CY] = x[strip(i), 0:CY]
         return carry
 
-    lax.fori_loop(1, STRIPS - 1, place, 0)
+    lax.fori_loop(1, STRIPS - 1, place, 0, unroll=True)
     first[0:8, 0:CY] = hrows[0]
     first[ROWS - 8 : ROWS, 0:CY] = hrows[1]
     for k in range(16):
@@ -416,32 +415,18 @@
         group = coefficients(0, a, w, 1)
         group = group + jnp.where(w > 0, coefficients(0, a, left, 0), 0.0)
         group = group + jnp.where(w < NW - 1, coefficients(0, a, right, 2), 0.0)
-        groups.append(group)
-    py[...] = prolonged(groups, sk, wk[...])
-
-    def total_at(i):
-        value = first[strip(i), :] + py[strip(i), :]
-        first[strip(i), :] = value
-        return hsum(value)
-
-    def residual(i, total):
-        value = gm[strip(i), :] - d3[strip(i), :] * first[strip(i), :] + total * (1.0 / 3.0)
-        return masked(value, valid4)
-
-    h0 = total_at(0)
-    h1 = total_at(1)
-    res[0:8, :] = jnp.where(wide_sub >= 4, residual(0, vsum(jnp.zeros_like(h0), h0, h1)), 0.0)
-
-    def residual_body(i, carry):
-        before, now = carry
-        after = total_at(i + 1)
-        res[strip(i), :] = residual(i, vsum(before, now, after))
-        return now, after
-
-    before, now = lax.fori_loop(1, STRIPS - 1, residual_body, (h0, h1))
-    res[ROWS - 8 : ROWS, :] = jnp.where(
-        wide_sub < 4, residual(STRIPS - 1, vsum(before, now, jnp.zeros_like(now))), 0.0
-    )
+        groups.append(jnp.where((lane % 16) // 4 == sub, group, 0.0))
+    py[...] = prolonged(groups, sk[...], wk[...])
+
+    def first_at(i):
+        value = first[rows_at(i), :] + py[rows_at(i), :] * (1.0 / 3.0)
+        first[rows_at(i), :] = value
+        return value
+
+    def residual(i, value, total):
+        res[rows_at(i), :] = inside(i, gm[rows_at(i), :] - d9[rows_at(i), :] * value + total, valid4)
+
+    stencil_strips(first_at, residual)
 
     rows[2] = jnp.broadcast_to(restrict(res), (8, 128))
     send_row(2)
@@ -455,46 +440,77 @@
     send_row(3)
 
     def add_local(i, carry):
-        first[strip(i), 0:CY] = first[strip(i), 0:CY] + x[strip(i), 0:CY]
+        first[strip(i), 0:CY] = (first[strip(i), 0:CY] + x[strip(i), 0:CY]) * 3.0
         return carry
 
-    lax.fori_loop(1, STRIPS - 1, add_local, 0)
+    lax.fori_loop(1, STRIPS - 1, add_local, 0, unroll=True)
+    base_copy = pltpu.make_async_copy(first.at[pl.ds(8, CX), pl.ds(0, CY)], base_hbm, store_sem.at[1])
+    base_copy.start()
     wait_rows(3)
     add_partials(1)
-    none = jnp.zeros((8, 128), F32)
-    py[0:CX, 0:CY] = prolonged([none, coefficients(1, s, w, 1), none], so, wk[:, 0:CY])
-
-    def add_coarse(i, carry):
-        first[strip(i + 1), 0:CY] = first[strip(i + 1), 0:CY] + py[strip(i), 0:CY]
-        return carry
-
-    lax.fori_loop(0, CX // 8, add_coarse, 0)
-    out_copy = pltpu.make_async_copy(first.at[pl.ds(8, CX), pl.ds(0, CY)], out_hbm, store_sem.at[1])
-    out_copy.start()
+    own_row = (lane % 16) // 4 == sub
+    mine_out[...] = jnp.where(own_row, coefficients(1, s, w, 1), 0.0)
     for which in range(4):
         wait_sent(which)
     for copy in margins:
         copy.wait_send()
     resid_copy.wait()
-    out_copy.wait()
+    base_copy.wait()
+
+
+PIECES = 4
+
+
+def finish(
+    base_hbm, resid_hbm, mine_hbm, stream_hbm, wall_hbm, out_hbm, resid_out,
+    base, resid, mine, stream_table, wall_table, small_sem, load_sem, store_sem,
+):
+    small = [
+        pltpu.make_async_copy(src, dst, small_sem.at[i])
+        for i, (src, dst) in enumerate([(mine_hbm, mine), (wall_hbm, wall_table), (stream_hbm, stream_table)])
+    ]
+    for copy in small:
+        copy.start()
+    parts = [pl.ds(i * (CX // PIECES), CX // PIECES) for i in range(PIECES)]
+    loads, stores = [], []
+    for k, (src, here, dst) in enumerate(((resid_hbm, resid, resid_out), (base_hbm, base, out_hbm))):
+        loads.append([pltpu.make_async_copy(src.at[p], here.at[p], load_sem.at[k, i]) for i, p in enumerate(parts)])
+        stores.append([pltpu.make_async_copy(here.at[p], dst.at[p], store_sem.at[k, i]) for i, p in enumerate(parts)])
+    for copy in loads[0] + loads[1]:
+        copy.start()
+    for copy in small:
+        copy.wait()
+    none = jnp.zeros((8, 128), F32)
+    coarse = prolonged([none, mine[...], none], stream_table[...], wall_table[...])
+    for i in range(PIECES):
+        loads[0][i].wait()
+        stores[0][i].start()
+    for i in range(PIECES):
+        rows = slice(i * (CX // PIECES), (i + 1) * (CX // PIECES))
+        loads[1][i].wait()
+        base[rows, :] = base[rows, :] + coarse[rows, :]
+        stores[1][i].start()
+    for copy in stores[0] + stores[1]:
+        copy.wait()
 
 
 def local(right_side, diagonal, coarse_inverse, owner_slot):
     phi_lanes, psi_rows, stream_k, own_k, wall_k = tables()
     field = jax.ShapeDtypeStruct((CX, CY), F32)
     anywhere = pl.BlockSpec(memory_space=pl.ANY)
+    in_vmem = pl.BlockSpec(memory_space=pltpu.VMEM)
     vmem = pltpu.VMEM
     dma = pltpu.SemaphoreType.DMA
     work = vmem((ROWS, COLS), F32)
-    return pl.pallas_call(
+    base, resid, mine = pl.pallas_call(
         kernel,
-        out_shape=(field, field),
-        in_specs=[anywhere] * 10,
-        out_specs=(anywhere, anywhere),
+        out_shape=(field, field, jax.ShapeDtypeStruct((8, 128), F32)),
+        in_specs=[anywhere] * 9,
+        out_specs=(anywhere, anywhere, in_vmem),
         scratch_shapes=[
-            vmem((2, ROWS, COLS), F32), work, work, work, work, work, work, work,
+            vmem((2, ROWS, COLS), F32), work, work, work, work, work, work, work, work,
             vmem((128, 512), F32), vmem((3 * CX, 128), F32), vmem((8, CY), F32),
-            vmem((ROWS, 128), BF16), vmem((CX, 128), BF16), vmem((256, COLS), BF16), vmem((1, DEVICES), jnp.int32),
+            vmem((ROWS, 128), BF16), vmem((256, COLS), BF16), vmem((1, DEVICES), jnp.int32),
             vmem((2, 32, 128), F32), vmem((2, 32, 128), F32), vmem((4, 2, 8, 128), F32),
             vmem((2, 16, 128), F32), vmem((2, 16, 128), F32), vmem((4, 8, 128), F32), vmem((2, 8, CY), F32),
             vmem((4, 8, 128), F32), vmem((4, DEVICES, 128), F32), vmem((2, 32, 128), F32),
@@ -502,13 +518,25 @@
             dma((10,)), dma((2, 8)), dma((2, 8)), dma((4,)), dma((4,)), dma((2,)),
         ],
         compiler_params=pltpu.CompilerParams(
-            collective_id=0, has_side_effects=True, vmem_limit_bytes=32 * 1024 * 1024
+            collective_id=0, has_side_effects=True, vmem_limit_bytes=60 * 1024 * 1024
         ),
         cost_estimate=pl.CostEstimate(flops=100_000_000, bytes_accessed=4_000_000, transcendentals=0),
     )(
         right_side, diagonal, coarse_inverse, owner_slot, owner_slot.reshape(1, DEVICES),
-        phi_lanes, psi_rows, stream_k, own_k, wall_k,
+        phi_lanes, psi_rows, stream_k, wall_k,
     )
+    return pl.pallas_call(
+        finish,
+        out_shape=(field, field),
+        in_specs=[anywhere] * 5,
+        out_specs=(anywhere, anywhere),
+        scratch_shapes=[
+            vmem((CX, CY), F32), vmem((CX, CY), F32), vmem((8, 128), F32), vmem((CX, 128), BF16), vmem((256, CY), BF16),
+            dma((3,)), dma((2, PIECES)), dma((2, PIECES)),
+        ],
+        compiler_params=pltpu.CompilerParams(vmem_limit_bytes=60 * 1024 * 1024),
+        cost_estimate=pl.CostEstimate(flops=50_000_000, bytes_accessed=3_000_000, transcendentals=0),
+    )(base, resid, mine, own_k, np.ascontiguousarray(wall_k[:, :CY]))
 
 
 def solution(mesh):

time: 82.8 us -> 54.4 us (0.66)
  Pallas kernels: 71.6 us -> 53.6 us
  local copies, waits for them, and re-layouts: 10.1 us -> 0 us
    pallas_call x1 -> x2, Pallas kernels: 71.6 us -> 53.6 us  [the longest x1 50.4 us: local(): pl.pallas_call(kernel, out_shape=(field, field, jax.ShapeDtypeStruct((8,...]
    unnamed x20 -> x0, local copies, waits for them, and re-layouts: 10.1 us -> none
where the time goes in v2:
time: 54.4 us; the launch traced here: 54.3 us
  Pallas kernels  53.6 us (99%)
  between operations  0.64 us (1%)
    pallas_call x1, Pallas kernels, local(): pl.pallas_call(kernel, out_shape=(field, field, jax.ShapeDtypeStruct((8,...  50.4 us
    pallas_call x1, Pallas kernels, local(): pl.pallas_call(finish, out_shape=(field, field), in_specs=[anywhere] * 5,...  3.23 us

profile of v2, /device:TPU:1, one launch (start us, length us, event | category | flops | bytes accessed | tf_op | source)
XLA Modules:
  0.0 54.3 jit_solution(13161532965708527205)
XLA Ops:
  0.6 50.4 %shard_map.113 = (f32[256,768]{1,0:T(8,128)}, f32[256,768]{1,0:T(8,128)}, f32[8,128]{1,0:T(8,128)}) custom-call(f32[256,768]{1,0:T(8,128)} %rhs_hbm.1, f32[256,768]{1,0:T(8,128)} %diag_hbm.1, f32[128,512]{1,0:T(8,128)} %inv_hbm.1, s32[256]{0:T(256)} %slot_hbm.1, s32[1,256]{1,0:T(1,128)} %bitcast.1, f32[768,128]{1,0:T(8,128)} %constant.12.clone.phi_hbm, ...), custom_call_target="tpu_custom_call" | custom-call | flops 100000000 | bytes 4000000 | tf_op jit(solution)/shard_map/pallas_call | solution.py:505
  51.0 3.2 %shard_map.114 = (f32[256,768]{1,0:T(8,128)}, f32[256,768]{1,0:T(8,128)}) custom-call(f32[256,768]{1,0:T(8,128)} %get-tuple-element.5.base_hbm, f32[256,768]{1,0:T(8,128)} %get-tuple-element.6.resid_hbm, f32[8,128]{1,0:T(8,128)} %get-tuple-element.7.mine_hbm, bf16[256,128]{1,0:T(8,128)(2,1)} %constant.16.clone.stream_hbm, ...), custom_call_target="tpu_custom_call" | custom-call | flops 50000000 | bytes 3000000 | tf_op jit(solution)/shard_map/pallas_call | solution.py:528

commit v3 on v2

--- a/solution.py
+++ b/solution.py
@@ -38,25 +38,92 @@
 
 
 def tables():
-    phi = np.cos(np.pi * (np.arange(CX) + 0.5)[None, :] * np.arange(4)[:, None] / CX)
-    psi = np.cos(np.pi * (np.arange(CY) + 0.5)[None, :] * np.arange(4)[:, None] / CY)
-    phi_lanes = np.repeat(phi[1:].reshape(3 * CX, 1), 128, axis=1).astype(np.float32)
-    psi_rows = np.concatenate([psi, psi]).astype(np.float32)
+    phi = np.cos(np.pi * (np.arange(CX) + 0.5)[None, :] * np.arange(7)[:, None] / CX)
+    psi = np.cos(np.pi * (np.arange(CY) + 0.5)[None, :] * np.arange(7)[:, None] / CY)
+    phi_lanes = np.repeat(phi[1:].reshape(6 * CX, 1), 128, axis=1).astype(np.float32)
+    psi_rows = np.concatenate([psi, psi[:1]]).astype(np.float32)
     stream = np.zeros((ROWS, 32), np.float32)
-    stream[0:8, 0:4] = phi[:, CX - 8 :].T
-    stream[8 : 8 + CX, 8:12] = phi.T
-    stream[8 + CX :, 16:20] = phi[:, :8].T
+    stream[0:8, 0:4] = phi[:4, CX - 8 :].T
+    stream[8 : 8 + CX, 8:12] = phi[:4].T
+    stream[8 + CX :, 16:20] = phi[:4, :8].T
     high, low = halves(stream)
     stream_k = np.concatenate([high, high, low, np.zeros_like(high)], axis=1)
     own_k = stream_k[8 : 8 + CX]
     wall = np.zeros((64, COLS), np.float32)
     for m in range(4):
-        wall[4 * m : 4 * m + 4, COLS - 64 :] = psi[:, CY - 64 :]
-        wall[16 + 4 * m : 20 + 4 * m, :CY] = psi
-        wall[32 + 4 * m : 36 + 4 * m, CY : CY + 64] = psi[:, :64]
+        wall[4 * m : 4 * m + 4, COLS - 64 :] = psi[:4, CY - 64 :]
+        wall[16 + 4 * m : 20 + 4 * m, :CY] = psi[:4]
+        wall[32 + 4 * m : 36 + 4 * m, CY : CY + 64] = psi[:4, :64]
     high, low = halves(wall)
     wall_k = np.concatenate([high, high, low, np.zeros_like(high)], axis=0)
     return phi_lanes, psi_rows, stream_k, own_k, wall_k
+
+
+EDGES = 20
+
+
+def coarse_tables():
+    phi = np.cos(np.pi * (np.arange(CX) + 0.5)[None, :] * np.arange(4)[:, None] / CX)
+    psi = np.cos(np.pi * (np.arange(CY) + 0.5)[None, :] * np.arange(4)[:, None] / CY)
+    lam = 1.0 + 2.0 * np.cos(np.pi * np.arange(4) / CX)
+    mu = 1.0 + 2.0 * np.cos(np.pi * np.arange(4) / CY)
+    p0, p1, q0, q1 = phi[:, 0], phi[:, -1], psi[:, 0], psi[:, -1]
+    nx, ny = (phi**2).sum(1), (psi**2).sum(1)
+    near = {(a, b): np.zeros((EDGES, 4, 4)) for a in (-1, 0, 1) for b in (-1, 0, 1)}
+    from_modes = np.zeros((4, 4, EDGES))
+    corner = {(0, 0): 16, (0, 1): 17, (1, 0): 18, (1, 1): 19}
+    ps, qs = (p0, p1), (q0, q1)
+    for n in range(4):
+        for side in (0, 1):
+            row = 4 * side + n
+            near[0, 0][row, :, n] -= mu[n] * ps[side]
+            near[1 if side == 0 else -1, 0][row, :, n] += mu[n] * ps[1 - side]
+            from_modes[:, n, row] += ps[side] * ny[n]
+    for m in range(4):
+        for side in (0, 1):
+            row = 8 + 4 * side + m
+            near[0, 0][row, m, :] -= lam[m] * qs[side]
+            near[0, 1 if side == 0 else -1][row, m, :] += lam[m] * qs[1 - side]
+            from_modes[m, :, row] += qs[side] * nx[m]
+    for (i, j), row in corner.items():
+        a, b = (1 if i == 0 else -1), (1 if j == 0 else -1)
+        near[0, 0][row] += np.outer(ps[i], qs[j])
+        near[a, 0][row] -= np.outer(ps[1 - i], qs[j])
+        near[0, b][row] -= np.outer(ps[i], qs[1 - j])
+        near[a, b][row] += np.outer(ps[1 - i], qs[1 - j])
+        from_modes[:, :, row] += np.outer(ps[i], qs[j])
+    near = {key: value.reshape(EDGES, 16) * (SCALE / 3.0) for key, value in near.items()}
+    from_modes = from_modes.reshape(16, EDGES)
+    smooth = np.outer(lam, mu).reshape(16) / 3.0
+    norm = np.outer(nx, ny).reshape(16)
+    mix = np.zeros((3, 128, 16))
+    mix[0, 0:16] = np.eye(16)
+    for side, b in enumerate((0, -1, 1)):
+        for place, a in enumerate((0, -1, 1)):
+            start = 16 + 36 * place
+            values = from_modes @ near[a, b]
+            if a == 0 and b == 0:
+                values = values - np.diag(SCALE * (3.0 - smooth) * norm)
+            mix[side, start : start + 20] = near[a, b]
+            for k in range(16):
+                mix[side, start + 20 + k] = values[(36 + k) % 16]
+    wide = np.concatenate([np.tile(mix[i], (1, 8)) for i in range(3)], axis=1).astype(np.float32)
+    high, low = halves(wide)
+    mix_k = np.concatenate([high, high, low], axis=0)
+    weights = np.zeros((52, 128), np.float32)
+    for k in range(16):
+        weights[k, k] = 3.0 * SCALE * smooth[k]
+        weights[16 + k, k] = -SCALE
+    for e in range(EDGES):
+        weights[32 + e, 16 + e] = 3.0
+    spread = np.zeros((128, 256), np.float32)
+    for k in range(16):
+        for j in range(16):
+            m, n, mm, nn = k // 4, k % 4, j // 4, j % 4
+            for p in (m + mm, abs(m - mm)):
+                for q in (n + nn, abs(n - nn)):
+                    spread[7 * p + q, 16 * k + j] += 0.25
+    return mix_k, np.repeat(weights, 8, axis=0), np.concatenate([spread, spread]).astype(BF16)
 
 
 def iota(shape, dim):
@@ -84,16 +151,23 @@
     return jnp.dot(stream_table, operand, preferred_element_type=F32)
 
 
+def tile16(value):
+    alike = jnp.where(iota((256, 128), 0) % 16 == iota((256, 128), 1) % 16, 1.0, 0.0).astype(BF16)
+    high, low = split(value)
+    both = jnp.concatenate([high, low], axis=1).astype(BF16)
+    return jnp.dot(both, alike, preferred_element_type=F32)
+
+
 def strip(i):
     return pl.ds(pl.multiple_of(i * 8, 8), 8)
 
 
 def kernel(
-    rhs_hbm, diag_hbm, inv_hbm, slot_hbm, slots_hbm, phi_hbm, psi_hbm, sk_hbm, wk_hbm,
+    rhs_hbm, diag_hbm, inv_hbm, slot_hbm, slots_hbm, phi_hbm, psi_hbm, sk_hbm, wk_hbm, mix_hbm, weights_hbm, spread_hbm,
     base_hbm, resid_hbm, mine_out,
-    ext, gm, d9, x, x2, u, first, res, py, inv, phi, psi, sk, wk, slots,
+    ext, gm, d9, x, x2, u, first, res, py, inv, phi, psi, sk, wk, mix, weights, spread, slots,
     colsend, colrecv, corners, hcolsend, hcolrecv, hcorners, hrows,
-    rows, bufs, ypk, slot,
+    row0, st, packed, cw, dbuf, row1, buf1, row2, buf2, ypk, onehot, block, diag_modes, slot,
     load_sem, msend, mrecv, asend, arecv, store_sem,
 ):
     s = lax.axis_index("stream")
@@ -126,8 +200,30 @@
         lax.fori_loop(0, 31, body, 0)
         some(jnp.int32(31), 7)
 
+    def stream_mates(act):
+        for d in (2, 3, 1, 0):
+            for flip in (1, 0):
+                if d or flip:
+                    act(((xl if flip == 0 else 1 - xl) * 4 + (ya + d) % 4, w))
+
+    def wall_mates(act):
+        for d in (4, 5, 3, 6, 2, 7, 1, 0):
+            for flip in (1, 0):
+                for other in (1, 0):
+                    if d or flip or other:
+                        x_part = (xh if flip == 0 else 1 - xh) * 16
+                        act((s, x_part + ((za + d) % 8) * 2 + (core if other == 0 else 1 - core)))
+
     barrier = pltpu.get_barrier_semaphore()
-    everyone(lambda to: pl.semaphore_signal(barrier, inc=1, device_id=to, device_id_type=MESH))
+
+    def greet(to):
+        pl.semaphore_signal(barrier, inc=1, device_id=to, device_id_type=MESH)
+
+    wall_mates(greet)
+    stream_mates(greet)
+    diagonals = [(up, left), (up, right), (down, left), (down, right)]
+    for to in diagonals:
+        greet(to)
 
     own = ext.at[:, pl.ds(8, CX), pl.ds(0, CY)]
     loads = [
@@ -143,6 +239,9 @@
                 (inv_hbm, inv),
                 (sk_hbm, sk),
                 (wk_hbm, wk),
+                (mix_hbm, mix),
+                (weights_hbm, weights),
+                (spread_hbm, spread),
             ]
         )
     ]
@@ -153,28 +252,31 @@
     sub = iota((8, 128), 0)
     lane16 = iota((16, 128), 1)
 
-    def restrict(ref):
+    def mode_sums(load, count):
         def body(i, sums):
-            f = ref[strip(i + 1), 0:CY]
+            f = load(i)
             new = [sums[0] + f]
-            for m in range(3):
+            for m in range(count - 1):
                 t = phi[pl.ds(pl.multiple_of(m * CX + i * 8, 8), 8), :]
                 new.append(sums[m + 1] + f * jnp.concatenate([t] * 6, axis=1))
             return tuple(new)
 
-        zero = jnp.zeros((8, CY), F32)
-        sums = lax.fori_loop(0, CX // 8, body, (zero,) * 4)
-        parts = []
-        for m in range(4):
-            for n in range(4):
-                value = sums[m] if n == 0 else sums[m] * psi[n : n + 1, :]
-                total = value[:, 0:128]
-                for t in range(1, 6):
-                    total = total + value[:, 128 * t : 128 * t + 128]
-                parts.append(total)
+        return lax.fori_loop(0, CX // 8, body, (jnp.zeros((8, CY), F32),) * count)
+
+    def fold(value):
+        total = value[:, 0:128]
+        for t in range(1, 6):
+            total = total + value[:, 128 * t : 128 * t + 128]
+        return total
+
+    def mode_parts(sums, count):
+        return [fold(v if n == 0 else v * psi[n : n + 1, :]) for v in sums for n in range(count)]
+
+    def gathered(parts, period):
         totals = lane_totals(jnp.concatenate(parts, axis=0))
-        keep = iota((128, 128), 0) // 8 == iota((128, 128), 1) % 16
-        return jnp.sum(jnp.where(keep, totals, 0.0), axis=0, keepdims=True) * SCALE
+        shape = totals.shape
+        keep = iota(shape, 0) // 8 == iota(shape, 1) % period
+        return jnp.sum(jnp.where(keep, totals, 0.0), axis=0, keepdims=True)
 
     def pack(ref):
         to_left = jnp.zeros((16, 128), F32)
@@ -206,32 +308,34 @@
             for i, ((src, dst), to) in enumerate(zip(pairs, targets, strict=True))
         ]
 
-    def send_row(which):
+    def sender(index, src, dst):
         def act(to):
             pltpu.make_async_remote_copy(
-                src_ref=rows.at[which, pl.ds(0, 1)], dst_ref=bufs.at[which, pl.ds(me, 1)],
-                send_sem=asend.at[which], recv_sem=arecv.at[which], device_id=to, device_id_type=MESH,
+                src_ref=src, dst_ref=dst, send_sem=asend.at[index], recv_sem=arecv.at[index],
+                device_id=to, device_id_type=MESH,
             ).start()
 
-        everyone(act)
-        pltpu.make_async_copy(
-            rows.at[which, pl.ds(0, 1)], bufs.at[which, pl.ds(me, 1)], arecv.at[which]
-        ).start()
-
-    def wait_rows(which):
-        pltpu.make_async_copy(bufs.at[which], bufs.at[which], arecv.at[which]).wait()
-
-    def wait_sent(which):
-        part = bufs.at[which, pl.ds(0, DEVICES - 1)]
-        pltpu.make_async_copy(part, part, asend.at[which]).wait()
-
-    def partial_values(c):
+        return act
+
+    def send(index, mates, src, dst):
+        mates(sender(index, src, dst))
+        pltpu.make_async_copy(src, dst, arecv.at[index]).start()
+
+    def wait_all(index, buf):
+        pltpu.make_async_copy(buf, buf, arecv.at[index]).wait()
+
+    def wait_sent(index, part):
+        pltpu.make_async_copy(part, part, asend.at[index]).wait()
+
+    def partial_values(c, tiled):
         at = iota((32, DEVICES), 0) + 32 * s
         pick = jnp.where(slots[...] == at, 1.0, 0.0)
         high, low = split(c)
         pick2 = jnp.concatenate([pick, pick], axis=1).astype(BF16)
         both = jnp.concatenate([high, low], axis=0).astype(BF16)
         ordered = jnp.dot(pick2, both, preferred_element_type=F32)
+        if not tiled:
+            ordered = tile16(ordered)
         keep = iota((32, 128), 1) // 16 == iota((32, 128), 0) % 8
         ordered = jnp.where(keep, ordered, 0.0)
         total = jnp.zeros((128, 128), F32)
@@ -242,9 +346,10 @@
         return jnp.sum(jnp.where(iota((128, 128), 0) == iota((128, 128), 1), sums, 0.0), axis=0, keepdims=True)
 
     def add_partials(which):
-        total = bufs[2 * which + 1, 0:32]
+        buf = buf1.at[0] if which == 0 else buf2
+        total = buf[0:32]
         for a in range(1, NS):
-            total = total + bufs[2 * which + 1, 32 * a : 32 * a + 32]
+            total = total + buf[32 * a : 32 * a + 32]
         ypk[which] = total
 
     def coefficients(which, a, b, place):
@@ -314,17 +419,21 @@
             stencil_strips(load, use)
             old, new = new, old
 
-    loads[0].wait()
-    loads[1].wait()
-    loads[2].wait()
-    rows[0] = jnp.broadcast_to(restrict(ext.at[0]), (8, 128))
+    for load in loads[:3]:
+        load.wait()
+    sums = mode_sums(lambda i: ext[0, strip(i + 1), 0:CY], 4)
+    first_residual = gathered(mode_parts(sums, 4), 16) * SCALE
+    lane1 = iota((1, 128), 1)
+    row0[0, 0:1] = jnp.where(lane1 // 16 == s, first_residual, 0.0)
     loads[3].wait()
+    sums = mode_sums(lambda i: ext[1, strip(i + 1), 0:CY], 7)
+    row0[0, 1:2] = gathered(mode_parts(sums, 7), 128)
     for f in range(2):
         a, b = pack(ext.at[f])
         colsend[0, 16 * f : 16 * f + 16] = a
         colsend[1, 16 * f : 16 * f + 16] = b
 
-    pl.semaphore_wait(barrier, DEVICES - 1)
+    pl.semaphore_wait(barrier, 7 + 31 + 4)
     top, bottom = pl.ds(8, 8), pl.ds(CX, 8)
     west, east, body_lanes = pl.ds(0, 128), pl.ds(CY - 128, 128), pl.ds(0, CY)
     margins = to_neighbours(
@@ -340,9 +449,22 @@
             (ext.at[:, bottom, east], corners.at[0]),
         ],
     )
+    send(0, stream_mates, row0, st.at[pl.ds(s, 1)])
     for copy in margins:
         copy.start()
-    send_row(0)
+    for load in loads[4:]:
+        load.wait()
+    at = iota((128, DEVICES), 0)
+    group_of = lax.shift_right_logical(slots[...], 3)
+    onehot[...] = jnp.where(jnp.logical_and(group_of == at % 32, at < 64), 1.0, 0.0).T
+    block[...] = jnp.where(lax.bitwise_and(slots[...], 7) == at // 16, 1.0, 0.0).T
+    wait_all(0, st)
+    total = st[0, 0:1]
+    for a in range(1, NS):
+        total = total + st[a, 0:1]
+    packed[...] = jnp.broadcast_to(total, (8, 128))
+    send(1, wall_mates, packed.at[pl.ds(0, 1)], cw.at[pl.ds(w, 1)])
+    send(2, wall_mates, st.at[:, pl.ds(1, 1), :], dbuf.at[:, pl.ds(w, 1), :])
     for copy in margins:
         copy.wait_recv()
 
@@ -384,11 +506,31 @@
     for copy in halos:
         copy.start()
 
-    for load in loads[4:]:
-        load.wait()
-    wait_rows(0)
-    rows[1] = jnp.broadcast_to(partial_values(bufs[0]), (8, 128))
-    send_row(1)
+    u_sums = mode_sums(lambda i: x[strip(i + 1), 0:CY], 4)
+    w_sums = mode_sums(lambda i: x[strip(i + 1), 0:CY] * d9[strip(i + 1), 0:CY], 4)
+    parts = mode_parts(u_sums, 4) + mode_parts(w_sums, 4)
+    for edge, here in ((x[8:16, 0:CY], sub == 0), (x[CX : CX + 8, 0:CY], sub == 7)):
+        parts += [jnp.where(here, p, 0.0) for p in mode_parts([edge], 4)]
+    parts += [jnp.where(lane == 0, v[:, 0:128], 0.0) for v in u_sums]
+    parts += [jnp.where(lane == 127, v[:, CY - 128 : CY], 0.0) for v in u_sums]
+    for edge, at_row in ((x[8:16, :], 0), (x[CX : CX + 8, :], 7)):
+        for tile, at_lane in ((edge[:, 0:128], 0), (edge[:, CY - 128 : CY], 127)):
+            parts.append(jnp.where(jnp.logical_and(sub == at_row, lane == at_lane), tile, 0.0))
+    totals = lane_totals(jnp.concatenate(parts, axis=0)) * weights[...]
+    moments = jnp.sum(totals, axis=0, keepdims=True)
+    moments = moments + jnp.where(lane1 < 16, first_residual, 0.0)
+    row1[1] = jnp.broadcast_to(moments, (8, 128))
+
+    wait_all(1, cw)
+    spread_rows = jnp.concatenate([cw[...]] * NS, axis=0)
+    own_lanes = iota((DEVICES, 128), 1) // 16 == iota((DEVICES, 128), 0) // NW
+    row1[0] = jnp.broadcast_to(partial_values(jnp.where(own_lanes, spread_rows, 0.0), False), (8, 128))
+    send(3, everyone, row1.at[:, pl.ds(0, 1), :], buf1.at[:, pl.ds(me, 1), :])
+
+    wait_all(2, dbuf)
+    high, low = split(dbuf[...].reshape(DEVICES, 128))
+    both = jnp.concatenate([high, low], axis=1).astype(BF16)
+    diag_modes[...] = jnp.dot(both, spread[...], preferred_element_type=F32) * (-SCALE)
 
     for copy in halos:
         copy.wait_recv()
@@ -408,8 +550,37 @@
     first[0:8, CY:COLS] = jnp.where(valid8, corner(hcorners[1], hcorners[0]), 0.0)
     first[ROWS - 8 : ROWS, CY:COLS] = jnp.where(valid8, corner(hcorners[3], hcorners[2]), 0.0)
 
-    wait_rows(1)
+    wait_all(3, buf1)
     add_partials(0)
+
+    high, low = split(ypk[0])
+    both = jnp.concatenate([high, low, jnp.zeros((64, 128), F32)], axis=0).astype(BF16)
+    values = jnp.dot(onehot[...].astype(BF16), both, preferred_element_type=F32) * block[...]
+    values = tile16(values)
+    known = buf1[1]
+    lanes = iota((DEVICES, 128), 1)
+    near = jnp.where(lanes < 36, known, jnp.where(lanes < 52, values, 0.0))
+    near = jnp.where(lanes >= 16, near, 0.0)
+    mixed = jnp.where(lanes < 16, known, near)
+    mixed = mixed + pltpu.roll(jnp.concatenate([near[-NW:], near[:-NW]], axis=0), 36, 1)
+    mixed = mixed + pltpu.roll(jnp.concatenate([near[NW:], near[:NW]], axis=0), 72, 1)
+    high, low = split(mixed)
+    both = jnp.concatenate([high, low, high], axis=1).astype(BF16)
+    sides = jnp.dot(both, mix[...], preferred_element_type=F32)
+    wall_row = iota((DEVICES, 128), 0) % NW
+    second_residual = sides[:, 0:128]
+    second_residual = second_residual + jnp.where(wall_row > 0, pltpu.roll(sides[:, 128:256], 1, 0), 0.0)
+    second_residual = second_residual + jnp.where(
+        wall_row < NW - 1, pltpu.roll(sides[:, 256:384], DEVICES - 1, 0), 0.0
+    )
+    products = [part for h in range(2) for part in split(values * diag_modes[:, 128 * h : 128 * h + 128])]
+    both = jnp.concatenate(products, axis=1).astype(BF16)
+    at = iota((512, 128), 0)
+    summed = jnp.where(8 * (at // 256) + (at % 128) // 16 == iota((512, 128), 1) % 16, 1.0, 0.0)
+    second_residual = second_residual + jnp.dot(both, summed.astype(BF16), preferred_element_type=F32)
+    row2[...] = jnp.broadcast_to(partial_values(second_residual, True), (8, 128))
+    send(4, everyone, row2.at[pl.ds(0, 1)], buf2.at[pl.ds(me, 1)])
+
     groups = []
     for a in (up, s, down):
         group = coefficients(0, a, w, 1)
@@ -428,16 +599,11 @@
 
     stencil_strips(first_at, residual)
 
-    rows[2] = jnp.broadcast_to(restrict(res), (8, 128))
-    send_row(2)
     resid_copy = pltpu.make_async_copy(res.at[pl.ds(8, CX), pl.ds(0, CY)], resid_hbm, store_sem.at[0])
     resid_copy.start()
     for copy in halos:
         copy.wait_send()
     chebyshev(res)
-    wait_rows(2)
-    rows[3] = jnp.broadcast_to(partial_values(bufs[2]), (8, 128))
-    send_row(3)
 
     def add_local(i, carry):
         first[strip(i), 0:CY] = (first[strip(i), 0:CY] + x[strip(i), 0:CY]) * 3.0
@@ -446,12 +612,15 @@
     lax.fori_loop(1, STRIPS - 1, add_local, 0, unroll=True)
     base_copy = pltpu.make_async_copy(first.at[pl.ds(8, CX), pl.ds(0, CY)], base_hbm, store_sem.at[1])
     base_copy.start()
-    wait_rows(3)
+    wait_all(4, buf2)
     add_partials(1)
     own_row = (lane % 16) // 4 == sub
     mine_out[...] = jnp.where(own_row, coefficients(1, s, w, 1), 0.0)
-    for which in range(4):
-        wait_sent(which)
+    wait_sent(0, st.at[pl.ds(0, 7)])
+    wait_sent(1, cw.at[pl.ds(0, 31)])
+    wait_sent(2, dbuf.at[:, pl.ds(0, 31), :])
+    wait_sent(3, buf1.at[:, pl.ds(0, DEVICES - 1), :])
+    wait_sent(4, buf2.at[pl.ds(0, DEVICES - 1)])
     for copy in margins:
         copy.wait_send()
     resid_copy.wait()
@@ -496,6 +665,7 @@
 
 def local(right_side, diagonal, coarse_inverse, owner_slot):
     phi_lanes, psi_rows, stream_k, own_k, wall_k = tables()
+    mix_k, moment_weights, spread_k = coarse_tables()
     field = jax.ShapeDtypeStruct((CX, CY), F32)
     anywhere = pl.BlockSpec(memory_space=pl.ANY)
     in_vmem = pl.BlockSpec(memory_space=pltpu.VMEM)
@@ -505,17 +675,21 @@
     base, resid, mine = pl.pallas_call(
         kernel,
         out_shape=(field, field, jax.ShapeDtypeStruct((8, 128), F32)),
-        in_specs=[anywhere] * 9,
+        in_specs=[anywhere] * 12,
         out_specs=(anywhere, anywhere, in_vmem),
         scratch_shapes=[
             vmem((2, ROWS, COLS), F32), work, work, work, work, work, work, work, work,
-            vmem((128, 512), F32), vmem((3 * CX, 128), F32), vmem((8, CY), F32),
-            vmem((ROWS, 128), BF16), vmem((256, COLS), BF16), vmem((1, DEVICES), jnp.int32),
+            vmem((128, 512), F32), vmem((6 * CX, 128), F32), vmem((8, CY), F32),
+            vmem((ROWS, 128), BF16), vmem((256, COLS), BF16),
+            vmem((384, 384), BF16), vmem((416, 128), F32), vmem((256, 256), BF16), vmem((1, DEVICES), jnp.int32),
             vmem((2, 32, 128), F32), vmem((2, 32, 128), F32), vmem((4, 2, 8, 128), F32),
             vmem((2, 16, 128), F32), vmem((2, 16, 128), F32), vmem((4, 8, 128), F32), vmem((2, 8, CY), F32),
-            vmem((4, 8, 128), F32), vmem((4, DEVICES, 128), F32), vmem((2, 32, 128), F32),
+            vmem((1, 2, 128), F32), vmem((NS, 2, 128), F32), vmem((8, 128), F32), vmem((NW, 128), F32),
+            vmem((NS, NW, 128), F32), vmem((2, 8, 128), F32), vmem((2, DEVICES, 128), F32),
+            vmem((8, 128), F32), vmem((DEVICES, 128), F32), vmem((2, NW, 128), F32),
+            vmem((DEVICES, 128), F32), vmem((DEVICES, 128), F32), vmem((DEVICES, 256), F32),
             pltpu.SMEM((DEVICES,), jnp.int32),
-            dma((10,)), dma((2, 8)), dma((2, 8)), dma((4,)), dma((4,)), dma((2,)),
+            dma((12,)), dma((2, 8)), dma((2, 8)), dma((5,)), dma((5,)), dma((2,)),
         ],
         compiler_params=pltpu.CompilerParams(
             collective_id=0, has_side_effects=True, vmem_limit_bytes=60 * 1024 * 1024
@@ -523,7 +697,7 @@
         cost_estimate=pl.CostEstimate(flops=100_000_000, bytes_accessed=4_000_000, transcendentals=0),
     )(
         right_side, diagonal, coarse_inverse, owner_slot, owner_slot.reshape(1, DEVICES),
-        phi_lanes, psi_rows, stream_k, wall_k,
+        phi_lanes, psi_rows, stream_k, wall_k, mix_k, moment_weights, spread_k,
     )
     return pl.pallas_call(
         finish,

time: 54.4 us -> 46.5 us (0.85)
  Pallas kernels: 53.6 us -> 45.8 us
    pallas_call x1, Pallas kernels: 50.4 us -> 42.6 us  [local(): pl.pallas_call(kernel, out_shape=(field, field, jax.ShapeDtypeStruct((8,...]
where the time goes in v3:
time: 46.5 us; the launch traced here: 46.4 us
  Pallas kernels  45.8 us (98%)
  between operations  0.64 us (1%)
    pallas_call x1, Pallas kernels, local(): pl.pallas_call(kernel, out_shape=(field, field, jax.ShapeDtypeStruct((8,...  42.6 us
    pallas_call x1, Pallas kernels, local(): pl.pallas_call(finish, out_shape=(field, field), in_specs=[anywhere] * 5,...  3.23 us

profile of v3, /device:TPU:1, one launch (start us, length us, event | category | flops | bytes accessed | tf_op | source)
XLA Modules:
  0.0 46.4 jit_solution(9635089864898724706)
XLA Ops:
  0.6 42.6 %shard_map.140 = (f32[256,768]{1,0:T(8,128)}, f32[256,768]{1,0:T(8,128)}, f32[8,128]{1,0:T(8,128)}) custom-call(f32[256,768]{1,0:T(8,128)} %rhs_hbm.1, f32[256,768]{1,0:T(8,128)} %diag_hbm.1, f32[128,512]{1,0:T(8,128)} %inv_hbm.1, s32[256]{0:T(256)} %slot_hbm.1, s32[1,256]{1,0:T(1,128)} %bitcast.1, f32[1536,128]{1,0:T(8,128)} %constant.18.clone.phi_hbm, ...), custom_call_target="tpu_custom_call" | custom-call | flops 100000000 | bytes 4000000 | tf_op jit(solution)/shard_map/pallas_call | solution.py:675
  43.2 3.2 %shard_map.141 = (f32[256,768]{1,0:T(8,128)}, f32[256,768]{1,0:T(8,128)}) custom-call(f32[256,768]{1,0:T(8,128)} %get-tuple-element.5.base_hbm, f32[256,768]{1,0:T(8,128)} %get-tuple-element.6.resid_hbm, f32[8,128]{1,0:T(8,128)} %get-tuple-element.7.mine_hbm, bf16[256,128]{1,0:T(8,128)(2,1)} %constant.25.clone.stream_hbm, ...), custom_call_target="tpu_custom_call" | custom-call | flops 50000000 | bytes 3000000 | tf_op jit(solution)/shard_map/pallas_call | solution.py:702

commit v4 on v3

--- a/solution.py
+++ b/solution.py
@@ -167,7 +167,7 @@
     base_hbm, resid_hbm, mine_out,
     ext, gm, d9, x, x2, u, first, res, py, inv, phi, psi, sk, wk, mix, weights, spread, slots,
     colsend, colrecv, corners, hcolsend, hcolrecv, hcorners, hrows,
-    row0, st, packed, cw, dbuf, row1, buf1, row2, buf2, ypk, onehot, block, diag_modes, slot,
+    rows, st, drow, dst, qst, qpack, cw, dbuf, qbuf, yw0, yw1, onehot, block, diag_modes, slot,
     load_sem, msend, mrecv, asend, arecv, store_sem,
 ):
     s = lax.axis_index("stream")
@@ -178,27 +178,6 @@
     xa = xh * 2 + xl
     up, down = (s + NS - 1) % NS, (s + 1) % NS
     left, right = (w + NW - 1) % NW, (w + 1) % NW
-
-    def around(k, n):
-        return n // 2 + (k % 2) * ((k + 1) // 2) - (1 - k % 2) * (k // 2)
-
-    def everyone(act):
-        ys = [(ya + d) % 4 for d in (2, 3, 1, 0)]
-
-        def some(k, count):
-            z = (za + around(k // 4, 8)) % 8
-            xx = (xa + around(k % 4, 4)) % 4
-            base_s = (xx % 2) * 4
-            base_w = (xx // 2) * 16 + z * 2
-            for j in range(count):
-                act((base_s + ys[j // 2], base_w + ((1 - core) if j % 2 == 0 else core)))
-
-        def body(k, carry):
-            some(k, 8)
-            return carry
-
-        lax.fori_loop(0, 31, body, 0)
-        some(jnp.int32(31), 7)
 
     def stream_mates(act):
         for d in (2, 3, 1, 0):
@@ -321,6 +300,15 @@
         mates(sender(index, src, dst))
         pltpu.make_async_copy(src, dst, arecv.at[index]).start()
 
+    def send_row(which):
+        send(2 * which, stream_mates, rows.at[which, pl.ds(0, 1)], st.at[which, pl.ds(s, 1)])
+
+    def forward_row(which, buf):
+        wait_all(2 * which, st.at[which])
+        total = jnp.sum(st[which], axis=0, keepdims=True)
+        rows[3 + which] = jnp.broadcast_to(total, (8, 128))
+        send(2 * which + 1, wall_mates, rows.at[3 + which, pl.ds(0, 1)], buf.at[pl.ds(w, 1)])
+
     def wait_all(index, buf):
         pltpu.make_async_copy(buf, buf, arecv.at[index]).wait()
 
@@ -345,16 +333,9 @@
         sums = lane_totals(total)
         return jnp.sum(jnp.where(iota((128, 128), 0) == iota((128, 128), 1), sums, 0.0), axis=0, keepdims=True)
 
-    def add_partials(which):
-        buf = buf1.at[0] if which == 0 else buf2
-        total = buf[0:32]
-        for a in range(1, NS):
-            total = total + buf[32 * a : 32 * a + 32]
-        ypk[which] = total
-
     def coefficients(which, a, b, place):
         mine = slot[a * NW + b]
-        row = ypk[which, pl.ds(lax.shift_right_logical(mine, 3), 1), :]
+        row = (yw1 if which else yw0)[pl.ds(lax.shift_right_logical(mine, 3), 1), :]
         shift = lax.bitwise_and(16 * place + 128 - 16 * lax.bitwise_and(mine, 7), 127)
         rolled = pltpu.roll(jnp.broadcast_to(row, (8, 128)), shift, 1)
         return jnp.where(lane // 16 == place, rolled, 0.0)
@@ -400,7 +381,7 @@
             return jnp.where(wide_sub < 4, value, 0.0)
         return value
 
-    def chebyshev(g):
+    def chebyshev(g, between=None):
         valid = tail_valid(4)
         old, new = x, x2
         for k, (a, b) in enumerate(sweep_factors()):
@@ -418,16 +399,16 @@
 
             stencil_strips(load, use)
             old, new = new, old
+            if k == 0 and between is not None:
+                between()
 
     for load in loads[:3]:
         load.wait()
     sums = mode_sums(lambda i: ext[0, strip(i + 1), 0:CY], 4)
     first_residual = gathered(mode_parts(sums, 4), 16) * SCALE
     lane1 = iota((1, 128), 1)
-    row0[0, 0:1] = jnp.where(lane1 // 16 == s, first_residual, 0.0)
+    rows[0] = jnp.broadcast_to(jnp.where(lane1 // 16 == s, first_residual, 0.0), (8, 128))
     loads[3].wait()
-    sums = mode_sums(lambda i: ext[1, strip(i + 1), 0:CY], 7)
-    row0[0, 1:2] = gathered(mode_parts(sums, 7), 128)
     for f in range(2):
         a, b = pack(ext.at[f])
         colsend[0, 16 * f : 16 * f + 16] = a
@@ -449,22 +430,21 @@
             (ext.at[:, bottom, east], corners.at[0]),
         ],
     )
-    send(0, stream_mates, row0, st.at[pl.ds(s, 1)])
+    send_row(0)
     for copy in margins:
         copy.start()
+    sums = mode_sums(lambda i: ext[1, strip(i + 1), 0:CY], 7)
+    drow[0] = gathered(mode_parts(sums, 7), 128)
+    send(6, stream_mates, drow, dst.at[pl.ds(s, 1)])
     for load in loads[4:]:
         load.wait()
     at = iota((128, DEVICES), 0)
     group_of = lax.shift_right_logical(slots[...], 3)
     onehot[...] = jnp.where(jnp.logical_and(group_of == at % 32, at < 64), 1.0, 0.0).T
     block[...] = jnp.where(lax.bitwise_and(slots[...], 7) == at // 16, 1.0, 0.0).T
-    wait_all(0, st)
-    total = st[0, 0:1]
-    for a in range(1, NS):
-        total = total + st[a, 0:1]
-    packed[...] = jnp.broadcast_to(total, (8, 128))
-    send(1, wall_mates, packed.at[pl.ds(0, 1)], cw.at[pl.ds(w, 1)])
-    send(2, wall_mates, st.at[:, pl.ds(1, 1), :], dbuf.at[:, pl.ds(w, 1), :])
+    forward_row(0, cw)
+    wait_all(6, dst)
+    send(7, wall_mates, dst, dbuf.at[:, pl.ds(w, 1), :])
     for copy in margins:
         copy.wait_recv()
 
@@ -519,18 +499,29 @@
     totals = lane_totals(jnp.concatenate(parts, axis=0)) * weights[...]
     moments = jnp.sum(totals, axis=0, keepdims=True)
     moments = moments + jnp.where(lane1 < 16, first_residual, 0.0)
-    row1[1] = jnp.broadcast_to(moments, (8, 128))
+    qpack[3] = moments
+    send(8, stream_mates, qpack.at[pl.ds(3, 1)], qst.at[pl.ds(s, 1)])
 
     wait_all(1, cw)
     spread_rows = jnp.concatenate([cw[...]] * NS, axis=0)
     own_lanes = iota((DEVICES, 128), 1) // 16 == iota((DEVICES, 128), 0) // NW
-    row1[0] = jnp.broadcast_to(partial_values(jnp.where(own_lanes, spread_rows, 0.0), False), (8, 128))
-    send(3, everyone, row1.at[:, pl.ds(0, 1), :], buf1.at[:, pl.ds(me, 1), :])
-
-    wait_all(2, dbuf)
+    rows[1] = jnp.broadcast_to(partial_values(jnp.where(own_lanes, spread_rows, 0.0), False), (8, 128))
+    send_row(1)
+
+    wait_all(8, qst)
+    for r in range(3):
+        total = jnp.zeros((1, 128), F32)
+        for a in range(3 * r, min(3 * r + 3, NS)):
+            value = jnp.broadcast_to(jnp.where(lane1 < 36, qst[a], 0.0), (8, 128))
+            total = total + (pltpu.roll(value, 40 * (a % 3), 1) if a % 3 else value)[0:1]
+        qpack[r] = total
+    send(9, wall_mates, qpack.at[pl.ds(0, 3)], qbuf.at[:, pl.ds(w, 1), :])
+
+    wait_all(7, dbuf)
     high, low = split(dbuf[...].reshape(DEVICES, 128))
     both = jnp.concatenate([high, low], axis=1).astype(BF16)
     diag_modes[...] = jnp.dot(both, spread[...], preferred_element_type=F32) * (-SCALE)
+    forward_row(1, yw0)
 
     for copy in halos:
         copy.wait_recv()
@@ -550,14 +541,18 @@
     first[0:8, CY:COLS] = jnp.where(valid8, corner(hcorners[1], hcorners[0]), 0.0)
     first[ROWS - 8 : ROWS, CY:COLS] = jnp.where(valid8, corner(hcorners[3], hcorners[2]), 0.0)
 
-    wait_all(3, buf1)
-    add_partials(0)
-
-    high, low = split(ypk[0])
+    wait_all(9, qbuf)
+    known = []
+    for a in range(NS):
+        value = qbuf[a // 3]
+        known.append(pltpu.roll(value, 128 - 40 * (a % 3), 1) if a % 3 else value)
+    known = jnp.concatenate(known, axis=0)
+    wait_all(3, yw0)
+
+    high, low = split(yw0[...])
     both = jnp.concatenate([high, low, jnp.zeros((64, 128), F32)], axis=0).astype(BF16)
     values = jnp.dot(onehot[...].astype(BF16), both, preferred_element_type=F32) * block[...]
     values = tile16(values)
-    known = buf1[1]
     lanes = iota((DEVICES, 128), 1)
     near = jnp.where(lanes < 36, known, jnp.where(lanes < 52, values, 0.0))
     near = jnp.where(lanes >= 16, near, 0.0)
@@ -578,8 +573,8 @@
     at = iota((512, 128), 0)
     summed = jnp.where(8 * (at // 256) + (at % 128) // 16 == iota((512, 128), 1) % 16, 1.0, 0.0)
     second_residual = second_residual + jnp.dot(both, summed.astype(BF16), preferred_element_type=F32)
-    row2[...] = jnp.broadcast_to(partial_values(second_residual, True), (8, 128))
-    send(4, everyone, row2.at[pl.ds(0, 1)], buf2.at[pl.ds(me, 1)])
+    rows[2] = jnp.broadcast_to(partial_values(second_residual, True), (8, 128))
+    send_row(2)
 
     groups = []
     for a in (up, s, down):
@@ -603,7 +598,7 @@
     resid_copy.start()
     for copy in halos:
         copy.wait_send()
-    chebyshev(res)
+    chebyshev(res, lambda: forward_row(2, yw1))
 
     def add_local(i, carry):
         first[strip(i), 0:CY] = (first[strip(i), 0:CY] + x[strip(i), 0:CY]) * 3.0
@@ -612,15 +607,16 @@
     lax.fori_loop(1, STRIPS - 1, add_local, 0, unroll=True)
     base_copy = pltpu.make_async_copy(first.at[pl.ds(8, CX), pl.ds(0, CY)], base_hbm, store_sem.at[1])
     base_copy.start()
-    wait_all(4, buf2)
-    add_partials(1)
+    wait_all(5, yw1)
     own_row = (lane % 16) // 4 == sub
     mine_out[...] = jnp.where(own_row, coefficients(1, s, w, 1), 0.0)
-    wait_sent(0, st.at[pl.ds(0, 7)])
-    wait_sent(1, cw.at[pl.ds(0, 31)])
-    wait_sent(2, dbuf.at[:, pl.ds(0, 31), :])
-    wait_sent(3, buf1.at[:, pl.ds(0, DEVICES - 1), :])
-    wait_sent(4, buf2.at[pl.ds(0, DEVICES - 1)])
+    for which, buf in enumerate((cw, yw0, yw1)):
+        wait_sent(2 * which, st.at[which, pl.ds(0, NS - 1)])
+        wait_sent(2 * which + 1, buf.at[pl.ds(0, NW - 1)])
+    wait_sent(6, dst.at[pl.ds(0, NS - 1)])
+    wait_sent(7, dbuf.at[:, pl.ds(0, NW - 1), :])
+    wait_sent(8, qst.at[pl.ds(0, NS - 1)])
+    wait_sent(9, qbuf.at[:, pl.ds(0, NW - 1), :])
     for copy in margins:
         copy.wait_send()
     resid_copy.wait()
@@ -684,12 +680,12 @@
             vmem((384, 384), BF16), vmem((416, 128), F32), vmem((256, 256), BF16), vmem((1, DEVICES), jnp.int32),
             vmem((2, 32, 128), F32), vmem((2, 32, 128), F32), vmem((4, 2, 8, 128), F32),
             vmem((2, 16, 128), F32), vmem((2, 16, 128), F32), vmem((4, 8, 128), F32), vmem((2, 8, CY), F32),
-            vmem((1, 2, 128), F32), vmem((NS, 2, 128), F32), vmem((8, 128), F32), vmem((NW, 128), F32),
-            vmem((NS, NW, 128), F32), vmem((2, 8, 128), F32), vmem((2, DEVICES, 128), F32),
-            vmem((8, 128), F32), vmem((DEVICES, 128), F32), vmem((2, NW, 128), F32),
+            vmem((6, 8, 128), F32), vmem((3, NS, 128), F32), vmem((1, 1, 128), F32), vmem((NS, 1, 128), F32),
+            vmem((NS, 1, 128), F32), vmem((4, 1, 128), F32), vmem((NW, 128), F32), vmem((NS, NW, 128), F32),
+            vmem((3, NW, 128), F32), vmem((NW, 128), F32), vmem((NW, 128), F32),
             vmem((DEVICES, 128), F32), vmem((DEVICES, 128), F32), vmem((DEVICES, 256), F32),
             pltpu.SMEM((DEVICES,), jnp.int32),
-            dma((12,)), dma((2, 8)), dma((2, 8)), dma((5,)), dma((5,)), dma((2,)),
+            dma((12,)), dma((2, 8)), dma((2, 8)), dma((10,)), dma((10,)), dma((2,)),
         ],
         compiler_params=pltpu.CompilerParams(
             collective_id=0, has_side_effects=True, vmem_limit_bytes=60 * 1024 * 1024

time: 46.5 us -> 47.1 us (1.013)
  Pallas kernels: 45.8 us -> 46.4 us
    pallas_call x1, Pallas kernels: 42.6 us -> 43.1 us  [local(): pl.pallas_call(kernel, out_shape=(field, field, jax.ShapeDtypeStruct((8,...]
where the time goes in v4:
time: 47.1 us; the launch traced here: 47 us
  Pallas kernels  46.4 us (99%)
  between operations  0.64 us (1%)
    pallas_call x1, Pallas kernels, local(): pl.pallas_call(kernel, out_shape=(field, field, jax.ShapeDtypeStruct((8,...  43.1 us
    pallas_call x1, Pallas kernels, local(): pl.pallas_call(finish, out_shape=(field, field), in_specs=[anywhere] * 5,...  3.23 us

profile of v4, /device:TPU:1, one launch (start us, length us, event | category | flops | bytes accessed | tf_op | source)
XLA Modules:
  0.0 47.0 jit_solution(5599272574983417444)
XLA Ops:
  0.6 43.1 %shard_map.140 = (f32[256,768]{1,0:T(8,128)}, f32[256,768]{1,0:T(8,128)}, f32[8,128]{1,0:T(8,128)}) custom-call(f32[256,768]{1,0:T(8,128)} %rhs_hbm.1, f32[256,768]{1,0:T(8,128)} %diag_hbm.1, f32[128,512]{1,0:T(8,128)} %inv_hbm.1, s32[256]{0:T(256)} %slot_hbm.1, s32[1,256]{1,0:T(1,128)} %bitcast.1, f32[1536,128]{1,0:T(8,128)} %constant.18.clone.phi_hbm, ...), custom_call_target="tpu_custom_call" | custom-call | flops 100000000 | bytes 4000000 | tf_op jit(solution)/shard_map/pallas_call | solution.py:671
  43.8 3.2 %shard_map.141 = (f32[256,768]{1,0:T(8,128)}, f32[256,768]{1,0:T(8,128)}) custom-call(f32[256,768]{1,0:T(8,128)} %get-tuple-element.5.base_hbm, f32[256,768]{1,0:T(8,128)} %get-tuple-element.6.resid_hbm, f32[8,128]{1,0:T(8,128)} %get-tuple-element.7.mine_hbm, bf16[256,128]{1,0:T(8,128)(2,1)} %constant.25.clone.stream_hbm, ...), custom_call_target="tpu_custom_call" | custom-call | flops 50000000 | bytes 3000000 | tf_op jit(solution)/shard_map/pallas_call | solution.py:698

commit v5 on v4

--- a/solution.py
+++ b/solution.py
@@ -167,7 +167,7 @@
     base_hbm, resid_hbm, mine_out,
     ext, gm, d9, x, x2, u, first, res, py, inv, phi, psi, sk, wk, mix, weights, spread, slots,
     colsend, colrecv, corners, hcolsend, hcolrecv, hcorners, hrows,
-    rows, st, drow, dst, qst, qpack, cw, dbuf, qbuf, yw0, yw1, onehot, block, diag_modes, slot,
+    rows, st, drow, dst, qst, qpack, dpack, cz, cw, dbuf, qbuf, yw0, yw1, onehot, block, diag_modes, slot,
     load_sem, msend, mrecv, asend, arecv, store_sem,
 ):
     s = lax.axis_index("stream")
@@ -193,15 +193,24 @@
                         x_part = (xh if flip == 0 else 1 - xh) * 16
                         act((s, x_part + ((za + d) % 8) * 2 + (core if other == 0 else 1 - core)))
 
+    def column_mates(act):
+        for d in (4, 5, 3, 6, 2, 7, 1, 0):
+            for other in (1, 0):
+                if d or other:
+                    act((s, xh * 16 + ((za + d) % 8) * 2 + (core if other == 0 else 1 - core)))
+
+    def across(act):
+        act((s, (1 - xh) * 16 + za * 2 + core))
+
     barrier = pltpu.get_barrier_semaphore()
 
     def greet(to):
         pl.semaphore_signal(barrier, inc=1, device_id=to, device_id_type=MESH)
 
-    wall_mates(greet)
+    column_mates(greet)
     stream_mates(greet)
-    diagonals = [(up, left), (up, right), (down, left), (down, right)]
-    for to in diagonals:
+    across(greet)
+    for to in [(up, left), (up, right), (down, left), (down, right), (s, left), (s, right)]:
         greet(to)
 
     own = ext.at[:, pl.ds(8, CX), pl.ds(0, CY)]
@@ -210,9 +219,10 @@
         for i, (src, dst) in enumerate(
             [
                 (rhs_hbm, own.at[0]),
-                (phi_hbm, phi),
+                (phi_hbm.at[pl.ds(0, 3 * CX)], phi.at[pl.ds(0, 3 * CX)]),
                 (psi_hbm, psi),
                 (diag_hbm, own.at[1]),
+                (phi_hbm.at[pl.ds(3 * CX, 3 * CX)], phi.at[pl.ds(3 * CX, 3 * CX)]),
                 (slot_hbm, slot),
                 (slots_hbm, slots),
                 (inv_hbm, inv),
@@ -230,17 +240,20 @@
     lane = iota((8, 128), 1)
     sub = iota((8, 128), 0)
     lane16 = iota((16, 128), 1)
+    lane1 = iota((1, 128), 1)
 
     def mode_sums(load, count):
-        def body(i, sums):
-            f = load(i)
-            new = [sums[0] + f]
-            for m in range(count - 1):
-                t = phi[pl.ds(pl.multiple_of(m * CX + i * 8, 8), 8), :]
-                new.append(sums[m + 1] + f * jnp.concatenate([t] * 6, axis=1))
-            return tuple(new)
-
-        return lax.fori_loop(0, CX // 8, body, (jnp.zeros((8, CY), F32),) * count)
+        def body(step, sums):
+            sums = list(sums)
+            for i in range(4):
+                f = load(step * 4 + i)
+                sums[0] = sums[0] + f
+                for m in range(count - 1):
+                    t = phi[pl.ds(pl.multiple_of(m * CX + (step * 4 + i) * 8, 8), 8), :]
+                    sums[m + 1] = sums[m + 1] + f * jnp.concatenate([t] * 6, axis=1)
+            return tuple(sums)
+
+        return lax.fori_loop(0, CX // 32, body, (jnp.zeros((8, CY), F32),) * count)
 
     def fold(value):
         total = value[:, 0:128]
@@ -303,11 +316,25 @@
     def send_row(which):
         send(2 * which, stream_mates, rows.at[which, pl.ds(0, 1)], st.at[which, pl.ds(s, 1)])
 
-    def forward_row(which, buf):
+    def forward_row(which, mates, dst):
         wait_all(2 * which, st.at[which])
         total = jnp.sum(st[which], axis=0, keepdims=True)
         rows[3 + which] = jnp.broadcast_to(total, (8, 128))
-        send(2 * which + 1, wall_mates, rows.at[3 + which, pl.ds(0, 1)], buf.at[pl.ds(w, 1)])
+        send(2 * which + 1, mates, rows.at[3 + which, pl.ds(0, 1)], dst)
+
+    def side_by_side(buf, per, width, used, r):
+        total = jnp.zeros((1, 128), F32)
+        for a in range(per * r, min(per * r + per, NS)):
+            value = jnp.broadcast_to(jnp.where(lane1 < used, buf[a], 0.0), (8, 128))
+            total = total + (pltpu.roll(value, width * (a % per), 1) if a % per else value)[0:1]
+        return total
+
+    def taken_apart(buf, per, width):
+        parts = []
+        for a in range(NS):
+            value = buf[a // per]
+            parts.append(pltpu.roll(value, 128 - width * (a % per), 1) if a % per else value)
+        return jnp.concatenate(parts, axis=0)
 
     def wait_all(index, buf):
         pltpu.make_async_copy(buf, buf, arecv.at[index]).wait()
@@ -381,7 +408,7 @@
             return jnp.where(wide_sub < 4, value, 0.0)
         return value
 
-    def chebyshev(g, between=None):
+    def chebyshev(g):
         valid = tail_valid(4)
         old, new = x, x2
         for k, (a, b) in enumerate(sweep_factors()):
@@ -399,14 +426,11 @@
 
             stencil_strips(load, use)
             old, new = new, old
-            if k == 0 and between is not None:
-                between()
 
     for load in loads[:3]:
         load.wait()
     sums = mode_sums(lambda i: ext[0, strip(i + 1), 0:CY], 4)
     first_residual = gathered(mode_parts(sums, 4), 16) * SCALE
-    lane1 = iota((1, 128), 1)
     rows[0] = jnp.broadcast_to(jnp.where(lane1 // 16 == s, first_residual, 0.0), (8, 128))
     loads[3].wait()
     for f in range(2):
@@ -414,7 +438,7 @@
         colsend[0, 16 * f : 16 * f + 16] = a
         colsend[1, 16 * f : 16 * f + 16] = b
 
-    pl.semaphore_wait(barrier, 7 + 31 + 4)
+    pl.semaphore_wait(barrier, 7 + 15 + 1 + 6)
     top, bottom = pl.ds(8, 8), pl.ds(CX, 8)
     west, east, body_lanes = pl.ds(0, 128), pl.ds(CY - 128, 128), pl.ds(0, CY)
     margins = to_neighbours(
@@ -433,18 +457,17 @@
     send_row(0)
     for copy in margins:
         copy.start()
+    loads[4].wait()
     sums = mode_sums(lambda i: ext[1, strip(i + 1), 0:CY], 7)
     drow[0] = gathered(mode_parts(sums, 7), 128)
     send(6, stream_mates, drow, dst.at[pl.ds(s, 1)])
-    for load in loads[4:]:
+    for load in loads[5:]:
         load.wait()
     at = iota((128, DEVICES), 0)
     group_of = lax.shift_right_logical(slots[...], 3)
     onehot[...] = jnp.where(jnp.logical_and(group_of == at % 32, at < 64), 1.0, 0.0).T
     block[...] = jnp.where(lax.bitwise_and(slots[...], 7) == at // 16, 1.0, 0.0).T
-    forward_row(0, cw)
-    wait_all(6, dst)
-    send(7, wall_mates, dst, dbuf.at[:, pl.ds(w, 1), :])
+    forward_row(0, column_mates, cz.at[pl.ds(w % 16, 1)])
     for copy in margins:
         copy.wait_recv()
 
@@ -466,6 +489,35 @@
     gm[0:8, :] = jnp.where(wide_sub >= 4, gm[0:8, :], 0.0)
     gm[ROWS - 8 : ROWS, :] = jnp.where(wide_sub < 4, gm[ROWS - 8 : ROWS, :], 0.0)
     chebyshev(gm)
+
+    wait_all(1, cz)
+    send(10, across, cz, cw.at[pl.ds(pl.multiple_of(xh * 16, 16), 16)])
+
+    u_sums = mode_sums(lambda i: x[strip(i + 1), 0:CY], 4)
+    w_sums = mode_sums(lambda i: x[strip(i + 1), 0:CY] * d9[strip(i + 1), 0:CY], 4)
+    parts = mode_parts(u_sums, 4) + mode_parts(w_sums, 4)
+    for edge, here in ((x[8:16, 0:CY], sub == 0), (x[CX : CX + 8, 0:CY], sub == 7)):
+        parts += [jnp.where(here, p, 0.0) for p in mode_parts([edge], 4)]
+    parts += [jnp.where(lane == 0, v[:, 0:128], 0.0) for v in u_sums]
+    parts += [jnp.where(lane == 127, v[:, CY - 128 : CY], 0.0) for v in u_sums]
+    for edge, at_row in ((x[8:16, :], 0), (x[CX : CX + 8, :], 7)):
+        for tile, at_lane in ((edge[:, 0:128], 0), (edge[:, CY - 128 : CY], 127)):
+            parts.append(jnp.where(jnp.logical_and(sub == at_row, lane == at_lane), tile, 0.0))
+    totals = lane_totals(jnp.concatenate(parts, axis=0)) * weights[...]
+    moments = jnp.sum(totals, axis=0, keepdims=True)
+    moments = moments + jnp.where(lane1 < 16, first_residual, 0.0)
+    qpack[3] = moments
+    send(8, stream_mates, qpack.at[pl.ds(3, 1)], qst.at[pl.ds(s, 1)])
+
+    wait_all(10, cw)
+    spread_rows = jnp.concatenate([cw[...]] * NS, axis=0)
+    own_lanes = iota((DEVICES, 128), 1) // 16 == iota((DEVICES, 128), 0) // NW
+    rows[1] = jnp.broadcast_to(partial_values(jnp.where(own_lanes, spread_rows, 0.0), False), (8, 128))
+    send_row(1)
+    wait_all(6, dst)
+    for r in range(4):
+        dpack[r] = side_by_side(dst, 2, 64, 49, r)
+    send(7, wall_mates, dpack, dbuf.at[:, pl.ds(w, 1), :])
 
     a, b = pack(x)
     hcolsend[0] = a
@@ -486,42 +538,11 @@
     for copy in halos:
         copy.start()
 
-    u_sums = mode_sums(lambda i: x[strip(i + 1), 0:CY], 4)
-    w_sums = mode_sums(lambda i: x[strip(i + 1), 0:CY] * d9[strip(i + 1), 0:CY], 4)
-    parts = mode_parts(u_sums, 4) + mode_parts(w_sums, 4)
-    for edge, here in ((x[8:16, 0:CY], sub == 0), (x[CX : CX + 8, 0:CY], sub == 7)):
-        parts += [jnp.where(here, p, 0.0) for p in mode_parts([edge], 4)]
-    parts += [jnp.where(lane == 0, v[:, 0:128], 0.0) for v in u_sums]
-    parts += [jnp.where(lane == 127, v[:, CY - 128 : CY], 0.0) for v in u_sums]
-    for edge, at_row in ((x[8:16, :], 0), (x[CX : CX + 8, :], 7)):
-        for tile, at_lane in ((edge[:, 0:128], 0), (edge[:, CY - 128 : CY], 127)):
-            parts.append(jnp.where(jnp.logical_and(sub == at_row, lane == at_lane), tile, 0.0))
-    totals = lane_totals(jnp.concatenate(parts, axis=0)) * weights[...]
-    moments = jnp.sum(totals, axis=0, keepdims=True)
-    moments = moments + jnp.where(lane1 < 16, first_residual, 0.0)
-    qpack[3] = moments
-    send(8, stream_mates, qpack.at[pl.ds(3, 1)], qst.at[pl.ds(s, 1)])
-
-    wait_all(1, cw)
-    spread_rows = jnp.concatenate([cw[...]] * NS, axis=0)
-    own_lanes = iota((DEVICES, 128), 1) // 16 == iota((DEVICES, 128), 0) // NW
-    rows[1] = jnp.broadcast_to(partial_values(jnp.where(own_lanes, spread_rows, 0.0), False), (8, 128))
-    send_row(1)
-
     wait_all(8, qst)
     for r in range(3):
-        total = jnp.zeros((1, 128), F32)
-        for a in range(3 * r, min(3 * r + 3, NS)):
-            value = jnp.broadcast_to(jnp.where(lane1 < 36, qst[a], 0.0), (8, 128))
-            total = total + (pltpu.roll(value, 40 * (a % 3), 1) if a % 3 else value)[0:1]
-        qpack[r] = total
+        qpack[r] = side_by_side(qst, 3, 40, 36, r)
     send(9, wall_mates, qpack.at[pl.ds(0, 3)], qbuf.at[:, pl.ds(w, 1), :])
-
-    wait_all(7, dbuf)
-    high, low = split(dbuf[...].reshape(DEVICES, 128))
-    both = jnp.concatenate([high, low], axis=1).astype(BF16)
-    diag_modes[...] = jnp.dot(both, spread[...], preferred_element_type=F32) * (-SCALE)
-    forward_row(1, yw0)
+    forward_row(1, wall_mates, yw0.at[pl.ds(w, 1)])
 
     for copy in halos:
         copy.wait_recv()
@@ -541,12 +562,13 @@
     first[0:8, CY:COLS] = jnp.where(valid8, corner(hcorners[1], hcorners[0]), 0.0)
     first[ROWS - 8 : ROWS, CY:COLS] = jnp.where(valid8, corner(hcorners[3], hcorners[2]), 0.0)
 
+    wait_all(7, dbuf)
+    diag = jnp.where(iota((DEVICES, 128), 1) < 64, taken_apart(dbuf, 2, 64), 0.0)
+    high, low = split(diag)
+    both = jnp.concatenate([high, low], axis=1).astype(BF16)
+    diag_modes[...] = jnp.dot(both, spread[...], preferred_element_type=F32) * (-SCALE)
     wait_all(9, qbuf)
-    known = []
-    for a in range(NS):
-        value = qbuf[a // 3]
-        known.append(pltpu.roll(value, 128 - 40 * (a % 3), 1) if a % 3 else value)
-    known = jnp.concatenate(known, axis=0)
+    known = taken_apart(qbuf, 3, 40)
     wait_all(3, yw0)
 
     high, low = split(yw0[...])
@@ -583,6 +605,7 @@
         group = group + jnp.where(w < NW - 1, coefficients(0, a, right, 2), 0.0)
         groups.append(jnp.where((lane % 16) // 4 == sub, group, 0.0))
     py[...] = prolonged(groups, sk[...], wk[...])
+    forward_row(2, wall_mates, yw1.at[pl.ds(w, 1)])
 
     def first_at(i):
         value = first[rows_at(i), :] + py[rows_at(i), :] * (1.0 / 3.0)
@@ -598,7 +621,7 @@
     resid_copy.start()
     for copy in halos:
         copy.wait_send()
-    chebyshev(res, lambda: forward_row(2, yw1))
+    chebyshev(res)
 
     def add_local(i, carry):
         first[strip(i), 0:CY] = (first[strip(i), 0:CY] + x[strip(i), 0:CY]) * 3.0
@@ -610,9 +633,10 @@
     wait_all(5, yw1)
     own_row = (lane % 16) // 4 == sub
     mine_out[...] = jnp.where(own_row, coefficients(1, s, w, 1), 0.0)
-    for which, buf in enumerate((cw, yw0, yw1)):
+    for which, part in enumerate((cz.at[pl.ds(0, 15)], yw0.at[pl.ds(0, NW - 1)], yw1.at[pl.ds(0, NW - 1)])):
         wait_sent(2 * which, st.at[which, pl.ds(0, NS - 1)])
-        wait_sent(2 * which + 1, buf.at[pl.ds(0, NW - 1)])
+        wait_sent(2 * which + 1, part)
+    wait_sent(10, cz)
     wait_sent(6, dst.at[pl.ds(0, NS - 1)])
     wait_sent(7, dbuf.at[:, pl.ds(0, NW - 1), :])
     wait_sent(8, qst.at[pl.ds(0, NS - 1)])
@@ -681,11 +705,11 @@
             vmem((2, 32, 128), F32), vmem((2, 32, 128), F32), vmem((4, 2, 8, 128), F32),
             vmem((2, 16, 128), F32), vmem((2, 16, 128), F32), vmem((4, 8, 128), F32), vmem((2, 8, CY), F32),
             vmem((6, 8, 128), F32), vmem((3, NS, 128), F32), vmem((1, 1, 128), F32), vmem((NS, 1, 128), F32),
-            vmem((NS, 1, 128), F32), vmem((4, 1, 128), F32), vmem((NW, 128), F32), vmem((NS, NW, 128), F32),
+            vmem((NS, 1, 128), F32), vmem((4, 1, 128), F32), vmem((4, 1, 128), F32), vmem((16, 128), F32), vmem((NW, 128), F32), vmem((4, NW, 128), F32),
             vmem((3, NW, 128), F32), vmem((NW, 128), F32), vmem((NW, 128), F32),
             vmem((DEVICES, 128), F32), vmem((DEVICES, 128), F32), vmem((DEVICES, 256), F32),
             pltpu.SMEM((DEVICES,), jnp.int32),
-            dma((12,)), dma((2, 8)), dma((2, 8)), dma((10,)), dma((10,)), dma((2,)),
+            dma((13,)), dma((2, 8)), dma((2, 8)), dma((11,)), dma((11,)), dma((2,)),
         ],
         compiler_params=pltpu.CompilerParams(
             collective_id=0, has_side_effects=True, vmem_limit_bytes=60 * 1024 * 1024

time: 47.1 us -> 48.1 us (1.021)
  Pallas kernels: 46.4 us -> 47.4 us
    pallas_call x1, Pallas kernels: 43.1 us -> 44.2 us  [local(): pl.pallas_call(kernel, out_shape=(field, field, jax.ShapeDtypeStruct((8,...]
where the time goes in v5:
time: 48.1 us; the launch traced here: 48 us
  Pallas kernels  47.4 us (99%)
  between operations  0.64 us (1%)
    pallas_call x1, Pallas kernels, local(): pl.pallas_call(kernel, out_shape=(field, field, jax.ShapeDtypeStruct((8,...  44.2 us
    pallas_call x1, Pallas kernels, local(): pl.pallas_call(finish, out_shape=(field, field), in_specs=[anywhere] * 5,...  3.23 us

profile of v5, /device:TPU:1, one launch (start us, length us, event | category | flops | bytes accessed | tf_op | source)
XLA Modules:
  0.0 48.0 jit_solution(5727612191271392638)
XLA Ops:
  0.6 44.2 %shard_map.140 = (f32[256,768]{1,0:T(8,128)}, f32[256,768]{1,0:T(8,128)}, f32[8,128]{1,0:T(8,128)}) custom-call(f32[256,768]{1,0:T(8,128)} %rhs_hbm.1, f32[256,768]{1,0:T(8,128)} %diag_hbm.1, f32[128,512]{1,0:T(8,128)} %inv_hbm.1, s32[256]{0:T(256)} %slot_hbm.1, s32[1,256]{1,0:T(1,128)} %bitcast.1, f32[1536,128]{1,0:T(8,128)} %constant.18.clone.phi_hbm, ...), custom_call_target="tpu_custom_call" | custom-call | flops 100000000 | bytes 4000000 | tf_op jit(solution)/shard_map/pallas_call | solution.py:695
  44.8 3.2 %shard_map.141 = (f32[256,768]{1,0:T(8,128)}, f32[256,768]{1,0:T(8,128)}) custom-call(f32[256,768]{1,0:T(8,128)} %get-tuple-element.5.base_hbm, f32[256,768]{1,0:T(8,128)} %get-tuple-element.6.resid_hbm, f32[8,128]{1,0:T(8,128)} %get-tuple-element.7.mine_hbm, bf16[256,128]{1,0:T(8,128)(2,1)} %constant.25.clone.stream_hbm, ...), custom_call_target="tpu_custom_call" | custom-call | flops 50000000 | bytes 3000000 | tf_op jit(solution)/shard_map/pallas_call | solution.py:722

commit v6 on v5

--- a/solution.py
+++ b/solution.py
@@ -167,7 +167,7 @@
     base_hbm, resid_hbm, mine_out,
     ext, gm, d9, x, x2, u, first, res, py, inv, phi, psi, sk, wk, mix, weights, spread, slots,
     colsend, colrecv, corners, hcolsend, hcolrecv, hcorners, hrows,
-    rows, st, drow, dst, qst, qpack, dpack, cz, cw, dbuf, qbuf, yw0, yw1, onehot, block, diag_modes, slot,
+    rows, st, drow, dst, qst, qpack, dpack, cw, dbuf, qbuf, yw0, yw1, all2, onehot, block, diag_modes, slot,
     load_sem, msend, mrecv, asend, arecv, store_sem,
 ):
     s = lax.axis_index("stream")
@@ -179,6 +179,28 @@
     up, down = (s + NS - 1) % NS, (s + 1) % NS
     left, right = (w + NW - 1) % NW, (w + 1) % NW
 
+    def around(k, n):
+        return n // 2 + (k % 2) * ((k + 1) // 2) - (1 - k % 2) * (k // 2)
+
+    def everyone(act):
+        xa = xh * 2 + xl
+        ys = [(ya + d) % 4 for d in (2, 3, 1, 0)]
+
+        def some(k, count):
+            z = (za + around(k // 4, 8)) % 8
+            xx = (xa + around(k % 4, 4)) % 4
+            base_s = (xx % 2) * 4
+            base_w = (xx // 2) * 16 + z * 2
+            for j in range(count):
+                act((base_s + ys[j // 2], base_w + ((1 - core) if j % 2 == 0 else core)))
+
+        def body(k, carry):
+            some(k, 8)
+            return carry
+
+        lax.fori_loop(0, 31, body, 0)
+        some(jnp.int32(31), 7)
+
     def stream_mates(act):
         for d in (2, 3, 1, 0):
             for flip in (1, 0):
@@ -193,24 +215,14 @@
                         x_part = (xh if flip == 0 else 1 - xh) * 16
                         act((s, x_part + ((za + d) % 8) * 2 + (core if other == 0 else 1 - core)))
 
-    def column_mates(act):
-        for d in (4, 5, 3, 6, 2, 7, 1, 0):
-            for other in (1, 0):
-                if d or other:
-                    act((s, xh * 16 + ((za + d) % 8) * 2 + (core if other == 0 else 1 - core)))
-
-    def across(act):
-        act((s, (1 - xh) * 16 + za * 2 + core))
-
     barrier = pltpu.get_barrier_semaphore()
 
     def greet(to):
         pl.semaphore_signal(barrier, inc=1, device_id=to, device_id_type=MESH)
 
-    column_mates(greet)
+    wall_mates(greet)
     stream_mates(greet)
-    across(greet)
-    for to in [(up, left), (up, right), (down, left), (down, right), (s, left), (s, right)]:
+    for to in [(up, left), (up, right), (down, left), (down, right)]:
         greet(to)
 
     own = ext.at[:, pl.ds(8, CX), pl.ds(0, CY)]
@@ -313,6 +325,16 @@
         mates(sender(index, src, dst))
         pltpu.make_async_copy(src, dst, arecv.at[index]).start()
 
+    def send_direct(which, buf):
+        send(2 * which, everyone, rows.at[which, pl.ds(0, 1)], buf.at[pl.ds(s * NW + w, 1)])
+
+    def sum_direct(which, buf, total_ref):
+        wait_all(2 * which, buf)
+        total = buf[0:NW]
+        for a in range(1, NS):
+            total = total + buf[NW * a : NW * a + NW]
+        total_ref[...] = total
+
     def send_row(which):
         send(2 * which, stream_mates, rows.at[which, pl.ds(0, 1)], st.at[which, pl.ds(s, 1)])
 
@@ -438,7 +460,7 @@
         colsend[0, 16 * f : 16 * f + 16] = a
         colsend[1, 16 * f : 16 * f + 16] = b
 
-    pl.semaphore_wait(barrier, 7 + 15 + 1 + 6)
+    pl.semaphore_wait(barrier, 7 + 31 + 4)
     top, bottom = pl.ds(8, 8), pl.ds(CX, 8)
     west, east, body_lanes = pl.ds(0, 128), pl.ds(CY - 128, 128), pl.ds(0, CY)
     margins = to_neighbours(
@@ -467,34 +489,48 @@
     group_of = lax.shift_right_logical(slots[...], 3)
     onehot[...] = jnp.where(jnp.logical_and(group_of == at % 32, at < 64), 1.0, 0.0).T
     block[...] = jnp.where(lax.bitwise_and(slots[...], 7) == at // 16, 1.0, 0.0).T
-    forward_row(0, column_mates, cz.at[pl.ds(w % 16, 1)])
+
+    def own_part(i, carry):
+        gm[strip(i), 0:CY] = ext[0, strip(i), 0:CY]
+        d9[strip(i), 0:CY] = ext[1, strip(i), 0:CY] * 3.0 + 9.0
+        return carry
+
+    lax.fori_loop(1, STRIPS - 1, own_part, 0, unroll=True)
+    forward_row(0, wall_mates, cw.at[pl.ds(w, 1)])
     for copy in margins:
         copy.wait_recv()
 
     valid4 = tail_valid(4)
-    for f in range(2):
-        from_right = colrecv[0, 16 * f : 16 * f + 16]
-        from_left = colrecv[1, 16 * f : 16 * f + 16]
-        for k in range(16):
-            ext[f, 8 + 16 * k : 24 + 16 * k, CY:COLS] = unpack(from_right, from_left, k)
-        ext[f, 0:8, CY:COLS] = corner(corners[1, f], corners[0, f])
-        ext[f, ROWS - 8 : ROWS, CY:COLS] = corner(corners[3, f], corners[2, f])
-
-    def prepare(i, carry):
-        gm[strip(i), :] = masked(ext[0, strip(i), :], valid4)
-        d9[strip(i), :] = ext[1, strip(i), :] * 3.0 + 9.0
-        return carry
-
-    lax.fori_loop(0, STRIPS, prepare, 0, unroll=True)
-    gm[0:8, :] = jnp.where(wide_sub >= 4, gm[0:8, :], 0.0)
-    gm[ROWS - 8 : ROWS, :] = jnp.where(wide_sub < 4, gm[ROWS - 8 : ROWS, :], 0.0)
+    two_strips = jnp.concatenate([valid4, valid4], axis=0)
+    for k in range(16):
+        here = slice(8 + 16 * k, 24 + 16 * k)
+        gm[here, CY:COLS] = jnp.where(two_strips, unpack(colrecv[0, 0:16], colrecv[1, 0:16], k), 0.0)
+        d9[here, CY:COLS] = unpack(colrecv[0, 16:32], colrecv[1, 16:32], k) * 3.0 + 9.0
+    for i, keep, right_at in ((0, sub >= 4, 1), (STRIPS - 1, sub < 4, 3)):
+        here = rows_at(i)
+        wide_keep = wide_sub[:, 0:CY] >= 4 if i == 0 else wide_sub[:, 0:CY] < 4
+        gm[here, 0:CY] = jnp.where(wide_keep, ext[0, here, 0:CY], 0.0)
+        d9[here, 0:CY] = ext[1, here, 0:CY] * 3.0 + 9.0
+        tail = corner(corners[right_at, 0], corners[right_at - 1, 0])
+        gm[here, CY:COLS] = jnp.where(jnp.logical_and(valid4, keep), tail, 0.0)
+        d9[here, CY:COLS] = corner(corners[right_at, 1], corners[right_at - 1, 1]) * 3.0 + 9.0
     chebyshev(gm)
 
-    wait_all(1, cz)
-    send(10, across, cz, cw.at[pl.ds(pl.multiple_of(xh * 16, 16), 16)])
-
-    u_sums = mode_sums(lambda i: x[strip(i + 1), 0:CY], 4)
-    w_sums = mode_sums(lambda i: x[strip(i + 1), 0:CY] * d9[strip(i + 1), 0:CY], 4)
+    def moment_body(step, sums):
+        sums = list(sums)
+        for k in range(2):
+            i = step * 2 + k
+            value = x[strip(i + 1), 0:CY]
+            weighted = value * d9[strip(i + 1), 0:CY]
+            sums[0], sums[4] = sums[0] + value, sums[4] + weighted
+            for m in range(1, 4):
+                t = phi[pl.ds(pl.multiple_of((m - 1) * CX + i * 8, 8), 8), :]
+                t = jnp.concatenate([t] * 6, axis=1)
+                sums[m], sums[4 + m] = sums[m] + value * t, sums[4 + m] + weighted * t
+        return tuple(sums)
+
+    sums = lax.fori_loop(0, CX // 16, moment_body, (jnp.zeros((8, CY), F32),) * 8)
+    u_sums, w_sums = sums[:4], sums[4:]
     parts = mode_parts(u_sums, 4) + mode_parts(w_sums, 4)
     for edge, here in ((x[8:16, 0:CY], sub == 0), (x[CX : CX + 8, 0:CY], sub == 7)):
         parts += [jnp.where(here, p, 0.0) for p in mode_parts([edge], 4)]
@@ -509,7 +545,7 @@
     qpack[3] = moments
     send(8, stream_mates, qpack.at[pl.ds(3, 1)], qst.at[pl.ds(s, 1)])
 
-    wait_all(10, cw)
+    wait_all(1, cw)
     spread_rows = jnp.concatenate([cw[...]] * NS, axis=0)
     own_lanes = iota((DEVICES, 128), 1) // 16 == iota((DEVICES, 128), 0) // NW
     rows[1] = jnp.broadcast_to(partial_values(jnp.where(own_lanes, spread_rows, 0.0), False), (8, 128))
@@ -596,7 +632,7 @@
     summed = jnp.where(8 * (at // 256) + (at % 128) // 16 == iota((512, 128), 1) % 16, 1.0, 0.0)
     second_residual = second_residual + jnp.dot(both, summed.astype(BF16), preferred_element_type=F32)
     rows[2] = jnp.broadcast_to(partial_values(second_residual, True), (8, 128))
-    send_row(2)
+    send_direct(2, all2)
 
     groups = []
     for a in (up, s, down):
@@ -605,7 +641,6 @@
         group = group + jnp.where(w < NW - 1, coefficients(0, a, right, 2), 0.0)
         groups.append(jnp.where((lane % 16) // 4 == sub, group, 0.0))
     py[...] = prolonged(groups, sk[...], wk[...])
-    forward_row(2, wall_mates, yw1.at[pl.ds(w, 1)])
 
     def first_at(i):
         value = first[rows_at(i), :] + py[rows_at(i), :] * (1.0 / 3.0)
@@ -630,13 +665,15 @@
     lax.fori_loop(1, STRIPS - 1, add_local, 0, unroll=True)
     base_copy = pltpu.make_async_copy(first.at[pl.ds(8, CX), pl.ds(0, CY)], base_hbm, store_sem.at[1])
     base_copy.start()
-    wait_all(5, yw1)
+    sum_direct(2, all2, yw1)
     own_row = (lane % 16) // 4 == sub
     mine_out[...] = jnp.where(own_row, coefficients(1, s, w, 1), 0.0)
-    for which, part in enumerate((cz.at[pl.ds(0, 15)], yw0.at[pl.ds(0, NW - 1)], yw1.at[pl.ds(0, NW - 1)])):
-        wait_sent(2 * which, st.at[which, pl.ds(0, NS - 1)])
-        wait_sent(2 * which + 1, part)
-    wait_sent(10, cz)
+    for which, part in enumerate((cw.at[pl.ds(0, NW - 1)], yw0.at[pl.ds(0, NW - 1)], None)):
+        if part is None:
+            wait_sent(2 * which, all2.at[pl.ds(0, DEVICES - 1)])
+        else:
+            wait_sent(2 * which, st.at[which, pl.ds(0, NS - 1)])
+            wait_sent(2 * which + 1, part)
     wait_sent(6, dst.at[pl.ds(0, NS - 1)])
     wait_sent(7, dbuf.at[:, pl.ds(0, NW - 1), :])
     wait_sent(8, qst.at[pl.ds(0, NS - 1)])
@@ -647,7 +684,7 @@
     base_copy.wait()
 
 
-PIECES = 4
+PIECES = 2
 
 
 def finish(
@@ -705,8 +742,9 @@
             vmem((2, 32, 128), F32), vmem((2, 32, 128), F32), vmem((4, 2, 8, 128), F32),
             vmem((2, 16, 128), F32), vmem((2, 16, 128), F32), vmem((4, 8, 128), F32), vmem((2, 8, CY), F32),
             vmem((6, 8, 128), F32), vmem((3, NS, 128), F32), vmem((1, 1, 128), F32), vmem((NS, 1, 128), F32),
-            vmem((NS, 1, 128), F32), vmem((4, 1, 128), F32), vmem((4, 1, 128), F32), vmem((16, 128), F32), vmem((NW, 128), F32), vmem((4, NW, 128), F32),
+            vmem((NS, 1, 128), F32), vmem((4, 1, 128), F32), vmem((4, 1, 128), F32), vmem((NW, 128), F32), vmem((4, NW, 128), F32),
             vmem((3, NW, 128), F32), vmem((NW, 128), F32), vmem((NW, 128), F32),
+            vmem((DEVICES, 128), F32),
             vmem((DEVICES, 128), F32), vmem((DEVICES, 128), F32), vmem((DEVICES, 256), F32),
             pltpu.SMEM((DEVICES,), jnp.int32),
             dma((13,)), dma((2, 8)), dma((2, 8)), dma((11,)), dma((11,)), dma((2,)),

time: 48.1 us -> 45.3 us (0.942)
  Pallas kernels: 47.4 us -> 44.6 us
    pallas_call x1, Pallas kernels: 44.2 us -> 41.6 us  [local(): pl.pallas_call(kernel, out_shape=(field, field, jax.ShapeDtypeStruct((8,...]
where the time goes in v6:
time: 45.3 us; the launch traced here: 45.2 us
  Pallas kernels  44.6 us (98%)
  between operations  0.64 us (1%)
    pallas_call x1, Pallas kernels, local(): pl.pallas_call(kernel, out_shape=(field, field, jax.ShapeDtypeStruct((8,...  41.6 us
    pallas_call x1, Pallas kernels, local(): pl.pallas_call(finish, out_shape=(field, field), in_specs=[anywhere] * 5,...  3 us

profile of v6, /device:TPU:1, one launch (start us, length us, event | category | flops | bytes accessed | tf_op | source)
XLA Modules:
  0.0 45.2 jit_solution(4423932664397732004)
XLA Ops:
  0.6 41.6 %shard_map.140 = (f32[256,768]{1,0:T(8,128)}, f32[256,768]{1,0:T(8,128)}, f32[8,128]{1,0:T(8,128)}) custom-call(f32[256,768]{1,0:T(8,128)} %rhs_hbm.1, f32[256,768]{1,0:T(8,128)} %diag_hbm.1, f32[128,512]{1,0:T(8,128)} %inv_hbm.1, s32[256]{0:T(256)} %slot_hbm.1, s32[1,256]{1,0:T(1,128)} %bitcast.1, f32[1536,128]{1,0:T(8,128)} %constant.18.clone.phi_hbm, ...), custom_call_target="tpu_custom_call" | custom-call | flops 100000000 | bytes 4000000 | tf_op jit(solution)/shard_map/pallas_call | solution.py:732
  42.2 3.0 %shard_map.141 = (f32[256,768]{1,0:T(8,128)}, f32[256,768]{1,0:T(8,128)}) custom-call(f32[256,768]{1,0:T(8,128)} %get-tuple-element.5.base_hbm, f32[256,768]{1,0:T(8,128)} %get-tuple-element.6.resid_hbm, f32[8,128]{1,0:T(8,128)} %get-tuple-element.7.mine_hbm, bf16[256,128]{1,0:T(8,128)(2,1)} %constant.25.clone.stream_hbm, ...), custom_call_target="tpu_custom_call" | custom-call | flops 50000000 | bytes 3000000 | tf_op jit(solution)/shard_map/pallas_call | solution.py:760

commit v7 on v6

--- a/solution.py
+++ b/solution.py
@@ -430,7 +430,7 @@
             return jnp.where(wide_sub < 4, value, 0.0)
         return value
 
-    def chebyshev(g):
+    def chebyshev(g, take=None):
         valid = tail_valid(4)
         old, new = x, x2
         for k, (a, b) in enumerate(sweep_factors()):
@@ -438,13 +438,18 @@
             def load(i, k=k, old=old):
                 return g[rows_at(i), :] * (1.0 / (3.0 * MIDDLE)) if k == 0 else old[rows_at(i), :]
 
-            def use(i, value, total, k=k, a=a, b=b, new=new):
+            last = k == DEG - 1 and take is not None
+
+            def use(i, value, total, k=k, a=a, b=b, new=new, last=last):
                 e = g[rows_at(i), :] - d9[rows_at(i), :] * value + total
                 step = a * (value if k == 0 else u[rows_at(i), :]) + (b / 3.0) * e
                 step = inside(i, step, valid)
                 if k < DEG - 1:
                     u[rows_at(i), :] = step
-                new[rows_at(i), :] = value + step
+                if last:
+                    take(i, value + step)
+                else:
+                    new[rows_at(i), :] = value + step
 
             stencil_strips(load, use)
             old, new = new, old
@@ -656,15 +661,23 @@
     resid_copy.start()
     for copy in halos:
         copy.wait_send()
-    chebyshev(res)
-
-    def add_local(i, carry):
-        first[strip(i), 0:CY] = (first[strip(i), 0:CY] + x[strip(i), 0:CY]) * 3.0
-        return carry
-
-    lax.fori_loop(1, STRIPS - 1, add_local, 0, unroll=True)
-    base_copy = pltpu.make_async_copy(first.at[pl.ds(8, CX), pl.ds(0, CY)], base_hbm, store_sem.at[1])
-    base_copy.start()
+    quarter = CX // 4
+    base_copies = [
+        pltpu.make_async_copy(
+            first.at[pl.ds(8 + quarter * p, quarter), pl.ds(0, CY)],
+            base_hbm.at[pl.ds(quarter * p, quarter)],
+            store_sem.at[1 + p],
+        )
+        for p in range(4)
+    ]
+
+    def add_local(i, value):
+        if 1 <= i <= CX // 8:
+            first[rows_at(i), 0:CY] = (first[rows_at(i), 0:CY] + value[:, 0:CY]) * 3.0
+            if i % (quarter // 8) == 0:
+                base_copies[i // (quarter // 8) - 1].start()
+
+    chebyshev(res, add_local)
     sum_direct(2, all2, yw1)
     own_row = (lane % 16) // 4 == sub
     mine_out[...] = jnp.where(own_row, coefficients(1, s, w, 1), 0.0)
@@ -681,7 +694,8 @@
     for copy in margins:
         copy.wait_send()
     resid_copy.wait()
-    base_copy.wait()
+    for copy in base_copies:
+        copy.wait()
 
 
 PIECES = 2
@@ -747,7 +761,7 @@
             vmem((DEVICES, 128), F32),
             vmem((DEVICES, 128), F32), vmem((DEVICES, 128), F32), vmem((DEVICES, 256), F32),
             pltpu.SMEM((DEVICES,), jnp.int32),
-            dma((13,)), dma((2, 8)), dma((2, 8)), dma((11,)), dma((11,)), dma((2,)),
+            dma((13,)), dma((2, 8)), dma((2, 8)), dma((11,)), dma((11,)), dma((5,)),
         ],
         compiler_params=pltpu.CompilerParams(
             collective_id=0, has_side_effects=True, vmem_limit_bytes=60 * 1024 * 1024

time: 45.3 us -> 45.2 us (level)
  no operation moved by 1% of the time
where the time goes in v7:
time: 45.2 us; the launch traced here: 45 us
  Pallas kernels  44.4 us (98%)
  between operations  0.64 us (1%)
    pallas_call x1, Pallas kernels, local(): pl.pallas_call(kernel, out_shape=(field, field, jax.ShapeDtypeStruct((8,...  41.4 us
    pallas_call x1, Pallas kernels, local(): pl.pallas_call(finish, out_shape=(field, field), in_specs=[anywhere] * 5,...  3 us

profile of v7, /device:TPU:1, one launch (start us, length us, event | category | flops | bytes accessed | tf_op | source)
XLA Modules:
  0.0 45.0 jit_solution(9798816710062540362)
XLA Ops:
  0.6 41.4 %shard_map.140 = (f32[256,768]{1,0:T(8,128)}, f32[256,768]{1,0:T(8,128)}, f32[8,128]{1,0:T(8,128)}) custom-call(f32[256,768]{1,0:T(8,128)} %rhs_hbm.1, f32[256,768]{1,0:T(8,128)} %diag_hbm.1, f32[128,512]{1,0:T(8,128)} %inv_hbm.1, s32[256]{0:T(256)} %slot_hbm.1, s32[1,256]{1,0:T(1,128)} %bitcast.1, f32[1536,128]{1,0:T(8,128)} %constant.18.clone.phi_hbm, ...), custom_call_target="tpu_custom_call" | custom-call | flops 100000000 | bytes 4000000 | tf_op jit(solution)/shard_map/pallas_call | solution.py:746
  42.0 3.0 %shard_map.141 = (f32[256,768]{1,0:T(8,128)}, f32[256,768]{1,0:T(8,128)}) custom-call(f32[256,768]{1,0:T(8,128)} %get-tuple-element.5.base_hbm, f32[256,768]{1,0:T(8,128)} %get-tuple-element.6.resid_hbm, f32[8,128]{1,0:T(8,128)} %get-tuple-element.7.mine_hbm, bf16[256,128]{1,0:T(8,128)(2,1)} %constant.25.clone.stream_hbm, ...), custom_call_target="tpu_custom_call" | custom-call | flops 50000000 | bytes 3000000 | tf_op jit(solution)/shard_map/pallas_call | solution.py:774

commit v8 on v6

--- a/solution.py
+++ b/solution.py
@@ -603,14 +603,19 @@
     high, low = split(diag)
     both = jnp.concatenate([high, low], axis=1).astype(BF16)
     diag_modes[...] = jnp.dot(both, spread[...], preferred_element_type=F32) * (-SCALE)
-    wait_all(9, qbuf)
-    known = taken_apart(qbuf, 3, 40)
     wait_all(3, yw0)
 
     high, low = split(yw0[...])
     both = jnp.concatenate([high, low, jnp.zeros((64, 128), F32)], axis=0).astype(BF16)
     values = jnp.dot(onehot[...].astype(BF16), both, preferred_element_type=F32) * block[...]
     values = tile16(values)
+    products = [part for h in range(2) for part in split(values * diag_modes[:, 128 * h : 128 * h + 128])]
+    both = jnp.concatenate(products, axis=1).astype(BF16)
+    at = iota((512, 128), 0)
+    summed = jnp.where(8 * (at // 256) + (at % 128) // 16 == iota((512, 128), 1) % 16, 1.0, 0.0)
+    from_diagonal = jnp.dot(both, summed.astype(BF16), preferred_element_type=F32)
+    wait_all(9, qbuf)
+    known = taken_apart(qbuf, 3, 40)
     lanes = iota((DEVICES, 128), 1)
     near = jnp.where(lanes < 36, known, jnp.where(lanes < 52, values, 0.0))
     near = jnp.where(lanes >= 16, near, 0.0)
@@ -621,16 +626,11 @@
     both = jnp.concatenate([high, low, high], axis=1).astype(BF16)
     sides = jnp.dot(both, mix[...], preferred_element_type=F32)
     wall_row = iota((DEVICES, 128), 0) % NW
-    second_residual = sides[:, 0:128]
+    second_residual = from_diagonal + sides[:, 0:128]
     second_residual = second_residual + jnp.where(wall_row > 0, pltpu.roll(sides[:, 128:256], 1, 0), 0.0)
     second_residual = second_residual + jnp.where(
         wall_row < NW - 1, pltpu.roll(sides[:, 256:384], DEVICES - 1, 0), 0.0
     )
-    products = [part for h in range(2) for part in split(values * diag_modes[:, 128 * h : 128 * h + 128])]
-    both = jnp.concatenate(products, axis=1).astype(BF16)
-    at = iota((512, 128), 0)
-    summed = jnp.where(8 * (at // 256) + (at % 128) // 16 == iota((512, 128), 1) % 16, 1.0, 0.0)
-    second_residual = second_residual + jnp.dot(both, summed.astype(BF16), preferred_element_type=F32)
     rows[2] = jnp.broadcast_to(partial_values(second_residual, True), (8, 128))
     send_direct(2, all2)
 

time: 45.3 us -> 45.5 us (level)
  no operation moved by 1% of the time
where the time goes in v8:
time: 45.5 us; the launch traced here: 45.3 us
  Pallas kernels  44.7 us (98%)
  between operations  0.64 us (1%)
    pallas_call x1, Pallas kernels, local(): pl.pallas_call(kernel, out_shape=(field, field, jax.ShapeDtypeStruct((8,...  41.7 us
    pallas_call x1, Pallas kernels, local(): pl.pallas_call(finish, out_shape=(field, field), in_specs=[anywhere] * 5,...  3 us

profile of v8, /device:TPU:1, one launch (start us, length us, event | category | flops | bytes accessed | tf_op | source)
XLA Modules:
  0.0 45.3 jit_solution(15636288128960654367)
XLA Ops:
  0.6 41.7 %shard_map.140 = (f32[256,768]{1,0:T(8,128)}, f32[256,768]{1,0:T(8,128)}, f32[8,128]{1,0:T(8,128)}) custom-call(f32[256,768]{1,0:T(8,128)} %rhs_hbm.1, f32[256,768]{1,0:T(8,128)} %diag_hbm.1, f32[128,512]{1,0:T(8,128)} %inv_hbm.1, s32[256]{0:T(256)} %slot_hbm.1, s32[1,256]{1,0:T(1,128)} %bitcast.1, f32[1536,128]{1,0:T(8,128)} %constant.18.clone.phi_hbm, ...), custom_call_target="tpu_custom_call" | custom-call | flops 100000000 | bytes 4000000 | tf_op jit(solution)/shard_map/pallas_call | solution.py:732
  42.3 3.0 %shard_map.141 = (f32[256,768]{1,0:T(8,128)}, f32[256,768]{1,0:T(8,128)}) custom-call(f32[256,768]{1,0:T(8,128)} %get-tuple-element.5.base_hbm, f32[256,768]{1,0:T(8,128)} %get-tuple-element.6.resid_hbm, f32[8,128]{1,0:T(8,128)} %get-tuple-element.7.mine_hbm, bf16[256,128]{1,0:T(8,128)(2,1)} %constant.25.clone.stream_hbm, ...), custom_call_target="tpu_custom_call" | custom-call | flops 50000000 | bytes 3000000 | tf_op jit(solution)/shard_map/pallas_call | solution.py:760
